TPU v7x, 128 devices: a whole 4x4x4 slice. The times are simulated.
128 devices in a mesh: dp: 4 (over z_hi, core), ctx: 32 (over z_lo, x, y).
Axes of the slice: x: 4, y: 4, z: 4 (z_hi: 2, z_lo: 2; z = z_hi * 2 + z_lo), core: 2. Of those that a mesh axis runs over, the one named last changes fastest.
Arguments:
- query: bfloat16 [4, 7168, 2560], P('dp', 'ctx'), may hold values from -12 to 12
- keys: bfloat16 [4, 7168, 512], P('dp', 'ctx'), may hold values from -12 to 12
- values: bfloat16 [4, 7168, 512], P('dp', 'ctx'), may hold values from -6 to 6
- section_order: int32 [64], replicated, may hold values from 0 to 63, each once
- kept_sections: int32 [4, 64], P('dp'), may hold values 0 or 1
- segment_ids: int32 [4, 7168], P('dp'), may hold values from 0 to 2, never falling along the last dimension, each value on 1 to 3584 neighbouring positions
- out_weight: bfloat16 [2560, 5120], P('ctx', 'dp'), may hold values from -0.59765625 to 0.59765625
Outputs:
- projected: bfloat16 [4, 7168, 5120], P('dp', 'ctx')
All inputs are finite; a program needn't handle non-finite values. No bound on the sum of `kept_sections` on one device may be relied on, other than what follows from the above.
Results may differ from a plain program's by a relative error of at most 0.0085.
Values may be sent and summed in bfloat16 or wider, within the bound.
No kernel may reach another device: no remote copies, remote signals or barrier semaphores. Data moves between devices by JAX's collectives and lax.ppermute only.
A program may use at most 192 MiB of HBM per device.

v0:
```python
import functools
import math

import jax
import jax.numpy as jnp
from jax import lax
from jax.experimental import pallas as pl
from jax.experimental.pallas import tpu as pltpu
from jax.sharding import Mesh, PartitionSpec as P

HD = 128
RING = 4
SHIFTS = (0, -1, 1, 2)
BLOCK_KEYS = 2048
TAIL_STEP = 256
ROW_TILE = 16


def shifted(array, axis, step, size=RING):
    return lax.ppermute(array, axis, [(i, (i + step) % size) for i in range(size)])


def ring_gather(array, axis):
    half = array.shape[0] // 2
    from_left = shifted(array, axis, 1)
    from_right = shifted(array, axis, -1)
    far_head = shifted(from_left[:half], axis, 1)
    far_tail = shifted(from_right[half:], axis, -1)
    return array, from_left, from_right, far_head, far_tail


def wrap(value):
    return lax.rem(value + RING, RING)


def attention_kernel(
    groups, sec, nsec, shifts, table, *refs
):
    count = len(shifts)
    q_refs, kv_refs, out_refs = refs[:count], refs[count : count + 9], refs[count + 9 : 2 * count + 9]
    held, q_all, out_all, acc, peak, sem = refs[2 * count + 9 :]
    base = 2 * nsec
    zl, x, y = table[base + 2], table[base + 3], table[base + 4]
    rows = nsec * sec
    factor = math.log2(math.e) / math.sqrt(HD)

    def copies(act):
        for side in range(2):
            own_zl = zl if side == 0 else 1 - zl
            for x_rel in range(4):
                abs_x = wrap(x + SHIFTS[x_rel])
                for y_rel in range(4):
                    abs_y = wrap(y + SHIFTS[y_rel])
                    if side == 1:
                        source = kv_refs[5 + x_rel].at[y_rel]
                    elif x_rel < 3:
                        source = kv_refs[x_rel].at[y_rel]
                    else:
                        source = kv_refs[3 + y_rel // 2].at[y_rel % 2]
                    for part in range(2):
                        section = ((own_zl * RING + abs_x) * RING + abs_y) * 2 + part
                        at = pl.multiple_of(table[section] * sec, ROW_TILE)
                        act(
                            source.at[pl.ds(part * sec, sec), :],
                            held.at[pl.ds(at, sec), pl.ds(0, 2 * HD)],
                        )

    copies(lambda a, b: pltpu.make_async_copy(a, b, sem).start())
    pad = held.shape[0] - rows
    held[pl.ds(rows, pad), pl.ds(0, 2 * HD)] = jnp.zeros((pad, 2 * HD), held.dtype)
    held[:, pl.ds(2 * HD, HD)] = jnp.ones((held.shape[0], HD), held.dtype)
    copies(lambda a, b: pltpu.make_async_copy(a, b, sem).wait())

    first, second = table[base], table[base + 1]

    def segment_start(pos):
        return jnp.where(pos >= second, second, jnp.where(pos >= first, first, 0))

    for piece in range(count):
        q_all[pl.ds(piece * 2 * sec, 2 * sec), :] = q_refs[piece][...]

    def one_section(index, _):
        piece, part = index // 2, lax.rem(index, 2)
        shift = shifts[0]
        for i in range(1, count):
            shift = jnp.where(piece == i, shifts[i], shift)
        section = ((zl * RING + x) * RING + wrap(y + shift)) * 2 + part
        place = table[section]
        begin = place * sec
        own_rows = pl.ds(pl.multiple_of(index * sec, ROW_TILE), sec)

        @pl.when(table[nsec + place] == 0)
        def _():
            out_all[own_rows, :] = jnp.zeros((sec, groups * HD), out_all.dtype)

        @pl.when(table[nsec + place] != 0)
        def _():
            key_first = segment_start(begin) // ROW_TILE * ROW_TILE
            last_start = segment_start(begin + sec - 1)
            full = (begin + sec - key_first) // BLOCK_KEYS
            tail_first = key_first + full * BLOCK_KEYS
            tail_steps = (begin + sec - tail_first + TAIL_STEP - 1) // TAIL_STEP
            peak[...] = jnp.full(peak.shape, -1e30, jnp.float32)
            acc[...] = jnp.zeros(acc.shape, jnp.float32)

            def step(first, width, masked):
                at = pl.multiple_of(first, ROW_TILE)
                keys = held[pl.ds(at, width), pl.ds(0, HD)]
                values = held[pl.ds(at, width), pl.ds(HD, 2 * HD)]
                if masked:
                    row_pos = begin + lax.broadcasted_iota(jnp.int32, (sec, 1), 0)
                    row_start = segment_start(row_pos)
                    key_pos = at + lax.broadcasted_iota(jnp.int32, (1, width), 1)
                    seen = (key_pos <= row_pos) & (key_pos >= row_start)
                def score(g):
                    got = lax.dot_general(
                        q_all[own_rows, pl.ds(g * HD, HD)],
                        keys,
                        (((1,), (1,)), ((), ())),
                        preferred_element_type=jnp.float32,
                    )
                    return jnp.where(seen, got, -1e30) if masked else got

                def weigh(g, got):
                    rows_g = pl.ds(g * sec, sec)
                    before = peak[rows_g, :]
                    top = jnp.maximum(before, jnp.max(got, axis=1, keepdims=True))
                    peak[rows_g, :] = top
                    scaled = top * factor
                    weights = jnp.exp2(
                        got * factor - jnp.concatenate([scaled] * (width // HD), axis=1)
                    ).astype(jnp.bfloat16)
                    return weights, jnp.exp2(before * factor - scaled)

                def add(g, weights, rescale):
                    rows_g = pl.ds(g * sec, sec)
                    acc[rows_g, :] = acc[rows_g, :] * jnp.concatenate(
                        [rescale, rescale], axis=1
                    ) + jnp.dot(weights, values, preferred_element_type=jnp.float32)

                ahead = score(0)
                waiting = None
                for g in range(groups):
                    got, ahead = ahead, score(g + 1) if g + 1 < groups else None
                    if waiting is not None:
                        add(g - 1, *waiting)
                    waiting = weigh(g, got)
                add(groups - 1, *waiting)

            def full_block(block, _):
                first = key_first + block * BLOCK_KEYS
                masked = (first < last_start) | (first + BLOCK_KEYS > begin)
                pl.when(masked)(lambda: step(first, BLOCK_KEYS, True))
                pl.when(jnp.logical_not(masked))(lambda: step(first, BLOCK_KEYS, False))
                return 0

            lax.fori_loop(0, full, full_block, 0)
            for steps in range(1, BLOCK_KEYS // TAIL_STEP + 1):
                pl.when(tail_steps == steps)(
                    lambda steps=steps: step(tail_first, steps * TAIL_STEP, True)
                )
            for g in range(groups):
                rows_g = pl.ds(g * sec, sec)
                out_all[own_rows, pl.ds(g * HD, HD)] = (
                    acc[rows_g, pl.ds(0, HD)] / acc[rows_g, pl.ds(HD, HD)]
                ).astype(out_all.dtype)

        return 0

    lax.fori_loop(0, 2 * count, one_section, 0)
    for piece in range(count):
        out_refs[piece][...] = out_all[pl.ds(piece * 2 * sec, 2 * sec), :]


def attention(table, shifts, q_pieces, kv_pieces, sec, nsec):
    groups = q_pieces[0].shape[1] // HD
    rows = nsec * sec
    count = len(shifts)
    smem = pl.BlockSpec(memory_space=pltpu.SMEM)
    vmem = pl.BlockSpec(memory_space=pltpu.VMEM)
    return pl.pallas_call(
        functools.partial(attention_kernel, groups, sec, nsec, shifts),
        out_shape=[jax.ShapeDtypeStruct(q.shape, q.dtype) for q in q_pieces],
        in_specs=[smem] + [vmem] * count + [pl.BlockSpec(memory_space=pl.ANY)] * 9,
        out_specs=[vmem] * count,
        scratch_shapes=[
            pltpu.VMEM((rows + TAIL_STEP, 3 * HD), jnp.bfloat16),
            pltpu.VMEM((2 * count * sec, groups * HD), jnp.bfloat16),
            pltpu.VMEM((2 * count * sec, groups * HD), jnp.bfloat16),
            pltpu.VMEM((groups * sec, 2 * HD), jnp.float32),
            pltpu.VMEM((groups * sec, HD), jnp.float32),
            pltpu.SemaphoreType.DMA,
        ],
        compiler_params=pltpu.CompilerParams(vmem_limit_bytes=48 * 2**20),
        cost_estimate=pl.CostEstimate(
            flops=count * 2 * 10**9,
            bytes_accessed=6 * 10**6,
            transcendentals=count * 4 * 10**6,
        ),
        name="attend",
    )(table, *q_pieces, *kv_pieces)


def project_kernel(base, table, *refs):
    att_refs, weights = refs[:8], refs[8]
    own_out, other_out, att = refs[9:]
    tok, wide = att_refs[0].shape

    @pl.when(pl.program_id(0) == 0)
    def _():
        for who in range(2):
            for j in range(4):
                head = wrap(table[base + 4] + SHIFTS[j])
                at = pl.multiple_of(head * wide, HD)
                att[pl.ds(who * tok, tok), pl.ds(at, wide)] = att_refs[4 * who + j][...]

    got = jnp.dot(att[...], weights[...], preferred_element_type=jnp.float32)
    got = got.astype(own_out.dtype)
    own_out[...] = got[:tok]
    other_out[0] = got[tok:]


def project(table, base, own_att, other_att, weights):
    tok, wide = own_att[0].shape
    rows, cols = RING * wide, weights.shape[1]
    piece = pl.BlockSpec((tok, wide), lambda i, *_: (0, 0))
    return pl.pallas_call(
        functools.partial(project_kernel, base),
        out_shape=[
            jax.ShapeDtypeStruct((tok, 4 * cols), jnp.bfloat16),
            jax.ShapeDtypeStruct((2, tok, cols), jnp.bfloat16),
        ],
        grid_spec=pltpu.PrefetchScalarGridSpec(
            num_scalar_prefetch=1,
            grid=(2,),
            in_specs=[piece] * 8 + [pl.BlockSpec((rows, cols), lambda i, *_: (i, 0))],
            out_specs=[
                pl.BlockSpec((tok, cols), lambda i, table: (0, i * 2 + table[base + 6])),
                pl.BlockSpec((1, tok, cols), lambda i, *_: (i, 0, 0)),
            ],
            scratch_shapes=[pltpu.VMEM((2 * tok, rows), jnp.bfloat16)],
        ),
        compiler_params=pltpu.CompilerParams(vmem_limit_bytes=48 * 2**20),
        cost_estimate=pl.CostEstimate(
            flops=6 * 10**9, bytes_accessed=18 * 10**6, transcendentals=0
        ),
        name="project",
    )(table, *own_att, *other_att, weights)


def merge_kernel(base, table, theirs, whole, out, sems):
    del whole
    cols = theirs.shape[2]

    def store(half):
        at = pl.multiple_of((half * 2 + 1 - table[base + 6]) * cols, HD)
        return pltpu.make_async_copy(theirs.at[half], out.at[:, pl.ds(at, cols)], sems.at[half])

    for half in range(2):
        store(half).start()
    for half in range(2):
        store(half).wait()


def merge(table, base, theirs, whole):
    anywhere = pl.BlockSpec(memory_space=pl.ANY)
    return pl.pallas_call(
        functools.partial(merge_kernel, base),
        out_shape=jax.ShapeDtypeStruct(whole.shape, whole.dtype),
        in_specs=[
            pl.BlockSpec(memory_space=pltpu.SMEM),
            pl.BlockSpec(memory_space=pltpu.VMEM),
            anywhere,
        ],
        out_specs=anywhere,
        scratch_shapes=[pltpu.SemaphoreType.DMA((2,))],
        input_output_aliases={2: 0},
        cost_estimate=pl.CostEstimate(flops=0, bytes_accessed=3 * 10**6, transcendentals=0),
        name="merge",
    )(table, theirs, whole)


def per_device(query, keys, values, section_order, kept_sections, segment_ids, out_weight):
    tok = query.shape[1]
    sec = tok // 2
    nsec = section_order.shape[0]
    zh, core = lax.axis_index("zh"), lax.axis_index("c")
    zl, x, y = lax.axis_index("zl"), lax.axis_index("x"), lax.axis_index("y")
    first, second = jnp.sum(segment_ids[0] < 1), jnp.sum(segment_ids[0] < 2)
    scalars = jnp.stack([first, second, zl, x, y, zh * 2 + zl, core]).astype(jnp.int32)
    table = jnp.concatenate([section_order, kept_sections[0], scalars])

    def head_slice(array, shift):
        wide = array.shape[2] // RING
        return lax.dynamic_slice_in_dim(array[0], wrap(y + shift) * wide, wide, 1)

    weights = lax.all_gather(out_weight, ("zh", "zl", "x", "y"), axis=0, tiled=True)

    pieces, q_pieces = [], []
    for shift in SHIFTS:
        kv = jnp.concatenate([head_slice(keys, -shift), head_slice(values, -shift)], axis=1)
        pieces.append(kv if shift == 0 else shifted(kv, "y", -shift))
    for shift in SHIFTS:
        q = head_slice(query, -shift)
        q_pieces.append(q if shift == 0 else shifted(q, "y", -shift))
    own = jnp.stack(pieces)
    far = shifted(own, "zl", 1, 2)
    near = ring_gather(own, "x")
    opposite = jnp.concatenate([near[3], near[4]], axis=0)
    far_all = (far, shifted(far, "x", 1), shifted(far, "x", -1), shifted(opposite, "zl", 1, 2))
    attended = attention(table, SHIFTS, q_pieces, near + far_all, sec, nsec)

    by_shift = dict(zip(SHIFTS, attended))
    back = {0: by_shift[0]}
    for shift in SHIFTS[1:]:
        back[wrap_static(-shift)] = shifted(by_shift[shift], "y", shift)
    own_att = [back[s] for s in SHIFTS]
    other_att = [shifted(a, "c", 1, 2) for a in own_att]
    base = 2 * nsec
    whole, for_other = project(table, base, own_att, other_att, weights)
    return merge(table, base, shifted(for_other, "c", 1, 2), whole)[None]


def wrap_static(shift):
    return 2 if shift in (2, -2) else shift


def solution(mesh):
    fine = Mesh(mesh.devices.reshape(2, 2, 2, 4, 4), ("zh", "c", "zl", "x", "y"))
    dp, ctx = ("zh", "c"), ("zl", "x", "y")
    return jax.shard_map(
        per_device,
        mesh=fine,
        in_specs=(
            P(dp, ctx, None),
            P(dp, ctx, None),
            P(dp, ctx, None),
            P(),
            P(dp, None),
            P(dp, None),
            P(ctx, dp),
        ),
        out_specs=P(dp, ctx, None),
        check_vma=False,
    )
```

profile of v0, /device:TPU:1, one launch (start us, length us, event | category | flops | bytes accessed | tf_op | source)
XLA Modules:
  0.0 149.9 jit_solution(13964108807038026516)
XLA Ops:
  8.4 2.2 %collective-permute-start.3 = (bf16[224,256]{1,0:T(8,128)(2,1)S(1)}, bf16[224,256]{1,0:T(8,128)(2,1)S(1)}, u32[]{:S(2)}, u32[]{:S(2)}) collective-permute-start(bf16[224,256]{1,0:T(8,128)(2,1)S(1)} %pad_maximum_fusion.2), channel_id=1, source_target_pairs={{0,1},{1,2},{2,3},{3,0},{4,5},{5,6},{6,7},{7,4},{8,9},{9,10},{10,1... | collective-permute-start | bytes 344072 | tf_op jit(solution)/shard_map/ppermute | solution.py:20
  12.1 1.7 %collective-permute-start.5 = (bf16[224,256]{1,0:T(8,128)(2,1)S(1)}, bf16[224,256]{1,0:T(8,128)(2,1)S(1)}, u32[]{:S(2)}, u32[]{:S(2)}) collective-permute-start(bf16[224,256]{1,0:T(8,128)(2,1)S(1)} %pad_maximum_fusion.4), channel_id=1, source_target_pairs={{0,2},{1,3},{2,0},{3,1},{4,6},{5,7},{6,4},{7,5},{8,10},{9,11},{10,... | collective-permute-start | bytes 344072 | tf_op jit(solution)/shard_map/ppermute | solution.py:20
  14.7 3.5 %collective-permute-done.5 = bf16[224,256]{1,0:T(8,128)(2,1)S(1)} collective-permute-done((bf16[224,256]{1,0:T(8,128)(2,1)S(1)}, bf16[224,256]{1,0:T(8,128)(2,1)S(1)}, u32[]{:S(2)}, u32[]{:S(2)}) %collective-permute-start.5) | collective-permute-done | bytes 114720 | tf_op jit(solution)/shard_map/ppermute | solution.py:20
  19.5 1.5 %collective-permute-start.7 = (bf16[4,224,256]{2,1,0:T(8,128)(2,1)S(1)}, bf16[4,224,256]{2,1,0:T(8,128)(2,1)S(1)}, u32[]{:S(2)}, u32[]{:S(2)}) collective-permute-start(bf16[4,224,256]{2,1,0:T(8,128)(2,1)S(1)} %pad_maximum_fusion.refs_4_), channel_id=1, source_target_pairs={{0,12},{4,0},{8,4},{12,8},{1,13},{5,1},{9,5},{13,9},{2,14},{6,2},{... | collective-permute-start | bytes 1376264 | tf_op jit(solution)/shard_map/ppermute | solution.py:20
  21.0 1.6 %collective-permute-start.10 = (bf16[4,224,256]{2,1,0:T(8,128)(2,1)S(1)}, bf16[4,224,256]{2,1,0:T(8,128)(2,1)S(1)}, u32[]{:S(2)}, u32[]{:S(2)}) collective-permute-start(bf16[4,224,256]{2,1,0:T(8,128)(2,1)S(1)} %pad_maximum_fusion.refs_4_), channel_id=1, source_target_pairs={{0,16},{16,0},{1,17},{17,1},{2,18},{18,2},{3,19},{19,3},{4,20},{20... | collective-permute-start | bytes 1376264 | tf_op jit(solution)/shard_map/ppermute | solution.py:20
  22.6 8.2 %collective-permute-done.6.refs_5_ = bf16[4,224,256]{2,1,0:T(8,128)(2,1)S(1)} collective-permute-done((bf16[4,224,256]{2,1,0:T(8,128)(2,1)S(1)}, bf16[4,224,256]{2,1,0:T(8,128)(2,1)S(1)}, u32[]{:S(2)}, u32[]{:S(2)}) %collective-permute-start.6) | collective-permute-done | bytes 458784 | tf_op jit(solution)/shard_map/ppermute | solution.py:20
  32.2 2.7 %collective-permute-start.9 = (bf16[2,224,256]{2,1,0:T(8,128)(2,1)}, bf16[2,224,256]{2,1,0:T(8,128)(2,1)S(1)}, u32[]{:S(2)}, u32[]{:S(2)}) collective-permute-start(bf16[2,224,256]{2,1,0:T(8,128)(2,1)} %slice.9), channel_id=1, source_target_pairs={{0,12},{4,0},{8,4},{12,8},{1,13},{5,1},{9,5},{13,9},{2,14},{6,2},{... | collective-permute-start | bytes 688136 | tf_op jit(solution)/shard_map/ppermute | solution.py:20
  34.9 2.2 %dynamic-slice_bitcast_fusion = (bf16[224,640]{1,0:T(8,128)(2,1)}, bf16[224,640]{1,0:T(8,128)(2,1)S(1)}, bf16[224,640]{1,0:T(8,128)(2,1)S(1)}, bf16[224,640]{1,0:T(8,128)(2,1)}) fusion(bf16[1,224,2560]{2,1,0:T(8,128)(2,1)} %param.7, s32[]{:T(128)S(6)} %select_n.31, s32[]{:T(128)S(6)} %select_n.29, s32[]{:T(128)S(6)} %select_n.28, s32[]{:T(128)S(6)} %select_n.30), kind=kLoop, calls=%fused_computation.2 | loop fusion | bytes 2293776 | tf_op jit(solution)/shard_map/dynamic_slice | solution.py:295
  37.2 2.7 %collective-permute-start.12 = (bf16[4,224,256]{2,1,0:T(8,128)(2,1)S(1)}, bf16[4,224,256]{2,1,0:T(8,128)(2,1)S(1)}, u32[]{:S(2)}, u32[]{:S(2)}) collective-permute-start(bf16[4,224,256]{2,1,0:T(8,128)(2,1)S(1)} %collective-permute-done.10.refs_9_), channel_id=1, source_target_pairs={{0,12},{4,0},{8,4},{12,8},{1,13},{5,1},{9,5},{13,9},{2,14},{6,2},{... | collective-permute-start | bytes 1376264 | tf_op jit(solution)/shard_map/ppermute | solution.py:20
  40.7 1.5 %collective-permute-start.13 = (bf16[4,224,256]{2,1,0:T(8,128)(2,1)}, bf16[4,224,256]{2,1,0:T(8,128)(2,1)}, u32[]{:S(2)}, u32[]{:S(2)}) collective-permute-start(bf16[4,224,256]{2,1,0:T(8,128)(2,1)} %pad_maximum_fusion.1), channel_id=1, source_target_pairs={{0,16},{16,0},{1,17},{17,1},{2,18},{18,2},{3,19},{19,3},{4,20},{20... | collective-permute-start | bytes 1376264 | tf_op jit(solution)/shard_map/ppermute | solution.py:20
  42.2 2.6 %collective-permute-start.1 = (bf16[224,640]{1,0:T(8,128)(2,1)}, bf16[224,640]{1,0:T(8,128)(2,1)}, u32[]{:S(2)}, u32[]{:S(2)}) collective-permute-start(bf16[224,640]{1,0:T(8,128)(2,1)} %get-tuple-element.22), channel_id=1, source_target_pairs={{0,3},{1,0},{2,1},{3,2},{4,7},{5,4},{6,5},{7,6},{8,11},{9,8},{10,9... | collective-permute-start | bytes 860168 | tf_op jit(solution)/shard_map/ppermute | solution.py:20
  47.5 7.8 %collective-permute-done.1.refs_2_ = bf16[224,640]{1,0:T(8,128)(2,1)} collective-permute-done((bf16[224,640]{1,0:T(8,128)(2,1)}, bf16[224,640]{1,0:T(8,128)(2,1)}, u32[]{:S(2)}, u32[]{:S(2)}) %collective-permute-start.1) | collective-permute-done | bytes 286752 | tf_op jit(solution)/shard_map/ppermute | solution.py:20
  55.3 4.0 %collective-permute-done.2.refs_3_ = bf16[224,640]{1,0:T(8,128)(2,1)} collective-permute-done((bf16[224,640]{1,0:T(8,128)(2,1)}, bf16[224,640]{1,0:T(8,128)(2,1)}, u32[]{:S(2)}, u32[]{:S(2)}) %collective-permute-start.2) | collective-permute-done | bytes 286752 | tf_op jit(solution)/shard_map/ppermute | solution.py:20
  60.3 16.8 %attend.1 = (bf16[224,640]{1,0:T(8,128)(2,1)S(1)}, bf16[224,640]{1,0:T(8,128)(2,1)S(1)}, bf16[224,640]{1,0:T(8,128)(2,1)S(1)}, bf16[224,640]{1,0:T(8,128)(2,1)S(1)}) custom-call(s32[135]{0:T(256)S(1)} %concatenate.18.table, bf16[224,640]{1,0:T(8,128)(2,1)S(1)} %get-tuple-element.21.refs_0_, bf16[224,640]{1,0:T(8,128)(2,1)S(1)} %copy-done.2, ...), custom_call_target="tpu_custom_call" | custom-call | flops 8000000000 | bytes 6000000 | tf_op jit(solution)/shard_map/attend/pallas_call | solution.py:181
  77.2 4.7 %collective-permute-start.14 = (bf16[224,640]{1,0:T(8,128)(2,1)S(1)}, bf16[224,640]{1,0:T(8,128)(2,1)S(1)}, u32[]{:S(2)}, u32[]{:S(2)}) collective-permute-start(bf16[224,640]{1,0:T(8,128)(2,1)S(1)} %get-tuple-element.12), channel_id=1, source_target_pairs={{0,1},{1,2},{2,3},{3,0},{4,5},{5,6},{6,7},{7,4},{8,9},{9,10},{10,1... | collective-permute-start | bytes 860168 | tf_op jit(solution)/shard_map/ppermute | solution.py:20
  83.8 5.2 %collective-permute-start.17 = (bf16[224,640]{1,0:T(8,128)(2,1)S(1)}, bf16[224,640]{1,0:T(8,128)(2,1)S(1)}, u32[]{:S(2)}, u32[]{:S(2)}) collective-permute-start(bf16[224,640]{1,0:T(8,128)(2,1)S(1)} %get-tuple-element.11.refs_0_), channel_id=1, source_target_pairs={{0,32},{32,0},{1,33},{33,1},{2,34},{34,2},{3,35},{35,3},{4,36},{36... | collective-permute-start | bytes 860168 | tf_op jit(solution)/shard_map/ppermute | solution.py:20
  89.7 4.9 %collective-permute-done.14.refs_1_ = bf16[224,640]{1,0:T(8,128)(2,1)S(1)} collective-permute-done((bf16[224,640]{1,0:T(8,128)(2,1)S(1)}, bf16[224,640]{1,0:T(8,128)(2,1)S(1)}, u32[]{:S(2)}, u32[]{:S(2)}) %collective-permute-start.14) | collective-permute-done | bytes 286752 | tf_op jit(solution)/shard_map/ppermute | solution.py:20
  94.6 6.3 %collective-permute-start.18 = (bf16[224,640]{1,0:T(8,128)(2,1)S(1)}, bf16[224,640]{1,0:T(8,128)(2,1)S(1)}, u32[]{:S(2)}, u32[]{:S(2)}) collective-permute-start(bf16[224,640]{1,0:T(8,128)(2,1)S(1)} %collective-permute-done.14.refs_1_), channel_id=1, source_target_pairs={{0,32},{32,0},{1,33},{33,1},{2,34},{34,2},{3,35},{35,3},{4,36},{36... | collective-permute-start | bytes 860168 | tf_op jit(solution)/shard_map/ppermute | solution.py:20
  101.9 6.0 %collective-permute-done.16.refs_3_ = bf16[224,640]{1,0:T(8,128)(2,1)S(1)} collective-permute-done((bf16[224,640]{1,0:T(8,128)(2,1)S(1)}, bf16[224,640]{1,0:T(8,128)(2,1)S(1)}, u32[]{:S(2)}, u32[]{:S(2)}) %collective-permute-start.16) | collective-permute-done | bytes 286752 | tf_op jit(solution)/shard_map/ppermute | solution.py:20
  107.9 5.5 %collective-permute-start.20 = (bf16[224,640]{1,0:T(8,128)(2,1)S(1)}, bf16[224,640]{1,0:T(8,128)(2,1)S(1)}, u32[]{:S(2)}, u32[]{:S(2)}) collective-permute-start(bf16[224,640]{1,0:T(8,128)(2,1)S(1)} %collective-permute-done.16.refs_3_), channel_id=1, source_target_pairs={{0,32},{32,0},{1,33},{33,1},{2,34},{34,2},{3,35},{35,3},{4,36},{36... | collective-permute-start | bytes 860168 | tf_op jit(solution)/shard_map/ppermute | solution.py:20
  114.6 10.4 %all-gather.2.cloned.1.call-done.refs_8_ = bf16[5120,1280]{1,0:T(8,128)(2,1)} async-done(((bf16[80,1280]{1,0:T(8,128)(2,1)}), bf16[5120,1280]{1,0:T(8,128)(2,1)}) %all-gather.2.cloned.1.call-update) | async-done | bytes 13107216 | tf_op jit(solution)/shard_map/all_gather | solution.py:297
  126.0 10.7 %project.1 = (bf16[224,5120]{1,0:T(8,128)(2,1)}, bf16[2,224,1280]{2,1,0:T(8,128)(2,1)S(1)}) custom-call(s32[135]{0:T(256)S(1)} %concatenate.18.table, bf16[224,640]{1,0:T(8,128)(2,1)S(1)} %copy-done.4, bf16[224,640]{1,0:T(8,128)(2,1)S(1)} %collective-permute-done.14.refs_1_, bf16[224,640]{1,0:T(8,128)(2,1)S(1)} %collective-permute-done.15.refs_2_, ...), custom_call_target="tpu_custom_call" | custom-call | flops 6000000000 | bytes 18000000 | tf_op jit(solution)/shard_map/project/pallas_call | solution.py:227
  137.3 2.4 %collective-permute-done.21.theirs = bf16[2,224,1280]{2,1,0:T(8,128)(2,1)S(1)} collective-permute-done((bf16[2,224,1280]{2,1,0:T(8,128)(2,1)S(1)}, bf16[2,224,1280]{2,1,0:T(8,128)(2,1)S(1)}, u32[]{:S(2)}, u32[]{:S(2)}) %collective-permute-start.21) | collective-permute-done | bytes 1146912 | tf_op jit(solution)/shard_map/ppermute | solution.py:20
  140.8 2.3 %merge.1 = bf16[224,5120]{1,0:T(8,128)(2,1)} custom-call(s32[135]{0:T(256)} %copy-done, bf16[2,224,1280]{2,1,0:T(8,128)(2,1)} %copy-done.5, bf16[224,5120]{1,0:T(8,128)(2,1)} %get-tuple-element.16.whole), custom_call_target="tpu_custom_call", output_to_operand_aliasing={{}: (2, {})} | custom-call | bytes 3000000 | tf_op jit(solution)/shard_map/merge/pallas_call | solution.py:267
  (56 shorter events, 19.0 us)
Async XLA Ops:
  6.5 118.5 %all-gather.2.cloned.1.call-start = ((), (), s32[]{:S(2)}) async-start(), calls=%async_computation | async-start | bytes 13312000 | tf_op jit(solution)/shard_map/all_gather | solution.py:297
  8.4 6.4 %collective-permute-start.3 = (bf16[224,256]{1,0:T(8,128)(2,1)S(1)}, bf16[224,256]{1,0:T(8,128)(2,1)S(1)}, u32[]{:S(2)}, u32[]{:S(2)}) collective-permute-start(bf16[224,256]{1,0:T(8,128)(2,1)S(1)} %pad_maximum_fusion.2), channel_id=1, source_target_pairs={{0,1},{1,2},{2,3},{3,0},{4,5},{5,6},{6,7},{7,4},{8,9},{9,10},{10,1... | collective-permute-start | bytes 344072 | tf_op jit(solution)/shard_map/ppermute | solution.py:20
  10.6 4.1 %collective-permute-start.4 = (bf16[224,256]{1,0:T(8,128)(2,1)S(1)}, bf16[224,256]{1,0:T(8,128)(2,1)S(1)}, u32[]{:S(2)}, u32[]{:S(2)}) collective-permute-start(bf16[224,256]{1,0:T(8,128)(2,1)S(1)} %pad_maximum_fusion.3), channel_id=1, source_target_pairs={{0,3},{1,0},{2,1},{3,2},{4,7},{5,4},{6,5},{7,6},{8,11},{9,8},{10,9... | collective-permute-start | bytes 344072 | tf_op jit(solution)/shard_map/ppermute | solution.py:20
  12.1 6.1 %collective-permute-start.5 = (bf16[224,256]{1,0:T(8,128)(2,1)S(1)}, bf16[224,256]{1,0:T(8,128)(2,1)S(1)}, u32[]{:S(2)}, u32[]{:S(2)}) collective-permute-start(bf16[224,256]{1,0:T(8,128)(2,1)S(1)} %pad_maximum_fusion.4), channel_id=1, source_target_pairs={{0,2},{1,3},{2,0},{3,1},{4,6},{5,7},{6,4},{7,5},{8,10},{9,11},{10,... | collective-permute-start | bytes 344072 | tf_op jit(solution)/shard_map/ppermute | solution.py:20
  18.3 12.5 %collective-permute-start.6 = (bf16[4,224,256]{2,1,0:T(8,128)(2,1)S(1)}, bf16[4,224,256]{2,1,0:T(8,128)(2,1)S(1)}, u32[]{:S(2)}, u32[]{:S(2)}) collective-permute-start(bf16[4,224,256]{2,1,0:T(8,128)(2,1)S(1)} %pad_maximum_fusion.refs_4_), channel_id=1, source_target_pairs={{0,4},{4,8},{8,12},{12,0},{1,5},{5,9},{9,13},{13,1},{2,6},{6,10},{... | collective-permute-start | bytes 1376264 | tf_op jit(solution)/shard_map/ppermute | solution.py:20
  19.5 12.0 %collective-permute-start.7 = (bf16[4,224,256]{2,1,0:T(8,128)(2,1)S(1)}, bf16[4,224,256]{2,1,0:T(8,128)(2,1)S(1)}, u32[]{:S(2)}, u32[]{:S(2)}) collective-permute-start(bf16[4,224,256]{2,1,0:T(8,128)(2,1)S(1)} %pad_maximum_fusion.refs_4_), channel_id=1, source_target_pairs={{0,12},{4,0},{8,4},{12,8},{1,13},{5,1},{9,5},{13,9},{2,14},{6,2},{... | collective-permute-start | bytes 1376264 | tf_op jit(solution)/shard_map/ppermute | solution.py:20
  21.0 16.0 %collective-permute-start.10 = (bf16[4,224,256]{2,1,0:T(8,128)(2,1)S(1)}, bf16[4,224,256]{2,1,0:T(8,128)(2,1)S(1)}, u32[]{:S(2)}, u32[]{:S(2)}) collective-permute-start(bf16[4,224,256]{2,1,0:T(8,128)(2,1)S(1)} %pad_maximum_fusion.refs_4_), channel_id=1, source_target_pairs={{0,16},{16,0},{1,17},{17,1},{2,18},{18,2},{3,19},{19,3},{4,20},{20... | collective-permute-start | bytes 1376264 | tf_op jit(solution)/shard_map/ppermute | solution.py:20
  31.5 8.3 %collective-permute-start.8 = (bf16[2,224,256]{2,1,0:T(8,128)(2,1)}, bf16[2,224,256]{2,1,0:T(8,128)(2,1)S(1)}, u32[]{:S(2)}, u32[]{:S(2)}) collective-permute-start(bf16[2,224,256]{2,1,0:T(8,128)(2,1)} %slice.8), channel_id=1, source_target_pairs={{0,4},{4,8},{8,12},{12,0},{1,5},{5,9},{9,13},{13,1},{2,6},{6,10},{... | collective-permute-start | bytes 688136 | tf_op jit(solution)/shard_map/ppermute | solution.py:20
  32.2 7.6 %collective-permute-start.9 = (bf16[2,224,256]{2,1,0:T(8,128)(2,1)}, bf16[2,224,256]{2,1,0:T(8,128)(2,1)S(1)}, u32[]{:S(2)}, u32[]{:S(2)}) collective-permute-start(bf16[2,224,256]{2,1,0:T(8,128)(2,1)} %slice.9), channel_id=1, source_target_pairs={{0,12},{4,0},{8,4},{12,8},{1,13},{5,1},{9,5},{13,9},{2,14},{6,2},{... | collective-permute-start | bytes 688136 | tf_op jit(solution)/shard_map/ppermute | solution.py:20
  37.1 7.7 %collective-permute-start = (bf16[224,640]{1,0:T(8,128)(2,1)S(1)}, bf16[224,640]{1,0:T(8,128)(2,1)S(1)}, u32[]{:S(2)}, u32[]{:S(2)}) collective-permute-start(bf16[224,640]{1,0:T(8,128)(2,1)S(1)} %get-tuple-element.20), channel_id=1, source_target_pairs={{0,1},{1,2},{2,3},{3,0},{4,5},{5,6},{6,7},{7,4},{8,9},{9,10},{10,1... | collective-permute-start | bytes 860168 | tf_op jit(solution)/shard_map/ppermute | solution.py:20
  37.1 22.3 %collective-permute-start.11 = (bf16[4,224,256]{2,1,0:T(8,128)(2,1)S(1)}, bf16[4,224,256]{2,1,0:T(8,128)(2,1)S(1)}, u32[]{:S(2)}, u32[]{:S(2)}) collective-permute-start(bf16[4,224,256]{2,1,0:T(8,128)(2,1)S(1)} %collective-permute-done.10.refs_9_), channel_id=1, source_target_pairs={{0,4},{4,8},{8,12},{12,0},{1,5},{5,9},{9,13},{13,1},{2,6},{6,10},{... | collective-permute-start | bytes 1376264 | tf_op jit(solution)/shard_map/ppermute | solution.py:20
  37.2 22.2 %collective-permute-start.12 = (bf16[4,224,256]{2,1,0:T(8,128)(2,1)S(1)}, bf16[4,224,256]{2,1,0:T(8,128)(2,1)S(1)}, u32[]{:S(2)}, u32[]{:S(2)}) collective-permute-start(bf16[4,224,256]{2,1,0:T(8,128)(2,1)S(1)} %collective-permute-done.10.refs_9_), channel_id=1, source_target_pairs={{0,12},{4,0},{8,4},{12,8},{1,13},{5,1},{9,5},{13,9},{2,14},{6,2},{... | collective-permute-start | bytes 1376264 | tf_op jit(solution)/shard_map/ppermute | solution.py:20
  40.7 18.7 %collective-permute-start.13 = (bf16[4,224,256]{2,1,0:T(8,128)(2,1)}, bf16[4,224,256]{2,1,0:T(8,128)(2,1)}, u32[]{:S(2)}, u32[]{:S(2)}) collective-permute-start(bf16[4,224,256]{2,1,0:T(8,128)(2,1)} %pad_maximum_fusion.1), channel_id=1, source_target_pairs={{0,16},{16,0},{1,17},{17,1},{2,18},{18,2},{3,19},{19,3},{4,20},{20... | collective-permute-start | bytes 1376264 | tf_op jit(solution)/shard_map/ppermute | solution.py:20
  42.2 13.2 %collective-permute-start.1 = (bf16[224,640]{1,0:T(8,128)(2,1)}, bf16[224,640]{1,0:T(8,128)(2,1)}, u32[]{:S(2)}, u32[]{:S(2)}) collective-permute-start(bf16[224,640]{1,0:T(8,128)(2,1)} %get-tuple-element.22), channel_id=1, source_target_pairs={{0,3},{1,0},{2,1},{3,2},{4,7},{5,4},{6,5},{7,6},{8,11},{9,8},{10,9... | collective-permute-start | bytes 860168 | tf_op jit(solution)/shard_map/ppermute | solution.py:20
  45.5 13.9 %collective-permute-start.2 = (bf16[224,640]{1,0:T(8,128)(2,1)}, bf16[224,640]{1,0:T(8,128)(2,1)}, u32[]{:S(2)}, u32[]{:S(2)}) collective-permute-start(bf16[224,640]{1,0:T(8,128)(2,1)} %get-tuple-element.19), channel_id=1, source_target_pairs={{0,2},{1,3},{2,0},{3,1},{4,6},{5,7},{6,4},{7,5},{8,10},{9,11},{10,... | collective-permute-start | bytes 860168 | tf_op jit(solution)/shard_map/ppermute | solution.py:20
  47.5 77.5 %copy-start = (s32[135]{0:T(256)}, s32[135]{0:T(256)S(1)}, u32[]{:S(2)}) copy-start(s32[135]{0:T(256)S(1)} %concatenate.18.table) | copy-start | bytes 1624
  77.2 17.5 %collective-permute-start.14 = (bf16[224,640]{1,0:T(8,128)(2,1)S(1)}, bf16[224,640]{1,0:T(8,128)(2,1)S(1)}, u32[]{:S(2)}, u32[]{:S(2)}) collective-permute-start(bf16[224,640]{1,0:T(8,128)(2,1)S(1)} %get-tuple-element.12), channel_id=1, source_target_pairs={{0,1},{1,2},{2,3},{3,0},{4,5},{5,6},{6,7},{7,4},{8,9},{9,10},{10,1... | collective-permute-start | bytes 860168 | tf_op jit(solution)/shard_map/ppermute | solution.py:20
  81.8 19.1 %collective-permute-start.15 = (bf16[224,640]{1,0:T(8,128)(2,1)S(1)}, bf16[224,640]{1,0:T(8,128)(2,1)S(1)}, u32[]{:S(2)}, u32[]{:S(2)}) collective-permute-start(bf16[224,640]{1,0:T(8,128)(2,1)S(1)} %get-tuple-element.13), channel_id=1, source_target_pairs={{0,3},{1,0},{2,1},{3,2},{4,7},{5,4},{6,5},{7,6},{8,11},{9,8},{10,9... | collective-permute-start | bytes 860168 | tf_op jit(solution)/shard_map/ppermute | solution.py:20
  82.7 25.2 %collective-permute-start.16 = (bf16[224,640]{1,0:T(8,128)(2,1)S(1)}, bf16[224,640]{1,0:T(8,128)(2,1)S(1)}, u32[]{:S(2)}, u32[]{:S(2)}) collective-permute-start(bf16[224,640]{1,0:T(8,128)(2,1)S(1)} %get-tuple-element.14), channel_id=1, source_target_pairs={{0,2},{1,3},{2,0},{3,1},{4,6},{5,7},{6,4},{7,5},{8,10},{9,11},{10,... | collective-permute-start | bytes 860168 | tf_op jit(solution)/shard_map/ppermute | solution.py:20
  83.8 29.6 %collective-permute-start.17 = (bf16[224,640]{1,0:T(8,128)(2,1)S(1)}, bf16[224,640]{1,0:T(8,128)(2,1)S(1)}, u32[]{:S(2)}, u32[]{:S(2)}) collective-permute-start(bf16[224,640]{1,0:T(8,128)(2,1)S(1)} %get-tuple-element.11.refs_0_), channel_id=1, source_target_pairs={{0,32},{32,0},{1,33},{33,1},{2,34},{34,2},{3,35},{35,3},{4,36},{36... | collective-permute-start | bytes 860168 | tf_op jit(solution)/shard_map/ppermute | solution.py:20
  94.6 18.7 %collective-permute-start.18 = (bf16[224,640]{1,0:T(8,128)(2,1)S(1)}, bf16[224,640]{1,0:T(8,128)(2,1)S(1)}, u32[]{:S(2)}, u32[]{:S(2)}) collective-permute-start(bf16[224,640]{1,0:T(8,128)(2,1)S(1)} %collective-permute-done.14.refs_1_), channel_id=1, source_target_pairs={{0,32},{32,0},{1,33},{33,1},{2,34},{34,2},{3,35},{35,3},{4,36},{36... | collective-permute-start | bytes 860168 | tf_op jit(solution)/shard_map/ppermute | solution.py:20
  100.9 12.4 %collective-permute-start.19 = (bf16[224,640]{1,0:T(8,128)(2,1)S(1)}, bf16[224,640]{1,0:T(8,128)(2,1)S(1)}, u32[]{:S(2)}, u32[]{:S(2)}) collective-permute-start(bf16[224,640]{1,0:T(8,128)(2,1)S(1)} %collective-permute-done.15.refs_2_), channel_id=1, source_target_pairs={{0,32},{32,0},{1,33},{33,1},{2,34},{34,2},{3,35},{35,3},{4,36},{36... | collective-permute-start | bytes 860168 | tf_op jit(solution)/shard_map/ppermute | solution.py:20
  107.9 6.7 %collective-permute-start.20 = (bf16[224,640]{1,0:T(8,128)(2,1)S(1)}, bf16[224,640]{1,0:T(8,128)(2,1)S(1)}, u32[]{:S(2)}, u32[]{:S(2)}) collective-permute-start(bf16[224,640]{1,0:T(8,128)(2,1)S(1)} %collective-permute-done.16.refs_3_), channel_id=1, source_target_pairs={{0,32},{32,0},{1,33},{33,1},{2,34},{34,2},{3,35},{35,3},{4,36},{36... | collective-permute-start | bytes 860168 | tf_op jit(solution)/shard_map/ppermute | solution.py:20
  136.7 3.1 %collective-permute-start.21 = (bf16[2,224,1280]{2,1,0:T(8,128)(2,1)S(1)}, bf16[2,224,1280]{2,1,0:T(8,128)(2,1)S(1)}, u32[]{:S(2)}, u32[]{:S(2)}) collective-permute-start(bf16[2,224,1280]{2,1,0:T(8,128)(2,1)S(1)} %get-tuple-element.15), channel_id=1, source_target_pairs={{0,32},{32,0},{1,33},{33,1},{2,34},{34,2},{3,35},{35,3},{4,36},{36... | collective-permute-start | bytes 3440648 | tf_op jit(solution)/shard_map/ppermute | solution.py:20
  (8 other events, 37.6 us)
Sparse Core Ops, SparseCore 0:
  10.2 114.7 all-gather.1
where the time goes:
time: 150 us
  waiting for transfers between devices  50.2 us (33%)
  starting transfers between devices  44.5 us (30%)
  Pallas kernels  29.8 us (20%)
  between operations  13.5 us (9%)
  local copies, waits for them, and re-layouts  10.3 us (7%)
  other arithmetic  1.65 us (1%)
    ppermute x22, starting transfers between devices, shifted(): lax.ppermute(array, axis, [(i, (i + step) % size) for i in range(size)])  44.5 us
    ppermute x22, waiting for transfers between devices, shifted(): lax.ppermute(array, axis, [(i, (i + step) % size) for i in range(size)])  39 us
    pallas_call x1, Pallas kernels, attention(): pl.pallas_call(functools.partial(attention_kernel, groups, sec, nsec, shi...  16.8 us
    pallas_call x1, Pallas kernels, project(): pl.pallas_call(functools.partial(project_kernel, base), out_shape=[jax.Sh...  10.7 us
    all_gather x1, waiting for transfers between devices, per_device(): lax.all_gather(out_weight, ('zh', 'zl', 'x', 'y'), axis=0, tiled=True)  10.4 us
    unnamed x18, local copies, waits for them, and re-layouts  4.35 us
    dynamic_slice x2, local copies, waits for them, and re-layouts, head_slice(): return lax.dynamic_slice_in_dim(array[0], wrap(y + shift) * wide, wide, 1)  3.25 us
  transfers between devices with their start and end apart: 23, of which 10 were waited for; matrix products, arithmetic and copies ran while one was open for 5% of the time, Pallas kernels for 11%

commit v1 on v0

--- a/solution.py
+++ b/solution.py
@@ -13,6 +13,7 @@
 SHIFTS = (0, -1, 1, 2)
 BLOCK_KEYS = 2048
 TAIL_STEP = 256
+CHUNK = 256
 ROW_TILE = 16
 
 
@@ -201,59 +202,80 @@
     )(table, *q_pieces, *kv_pieces)
 
 
-def project_kernel(base, table, *refs):
+def project_kernel(*refs):
     att_refs, weights = refs[:8], refs[8]
-    own_out, other_out, att = refs[9:]
+    whole, other_out, att, held, own, sems = refs[9:]
     tok, wide = att_refs[0].shape
-
-    @pl.when(pl.program_id(0) == 0)
-    def _():
-        for who in range(2):
-            for j in range(4):
-                head = wrap(table[base + 4] + SHIFTS[j])
-                at = pl.multiple_of(head * wide, HD)
-                att[pl.ds(who * tok, tok), pl.ds(at, wide)] = att_refs[4 * who + j][...]
-
-    got = jnp.dot(att[...], weights[...], preferred_element_type=jnp.float32)
-    got = got.astype(own_out.dtype)
-    own_out[...] = got[:tok]
-    other_out[0] = got[tok:]
-
-
-def project(table, base, own_att, other_att, weights):
+    cols = weights.shape[1]
+    rows = RING * wide
+    chunks = cols // CHUNK
+    y, core = lax.axis_index("y"), lax.axis_index("c")
+
+    def load(half, i):
+        at = (pl.ds(half * rows, rows), pl.ds(i * CHUNK, CHUNK))
+        return pltpu.make_async_copy(weights.at[at], held.at[at], sems.at[half * chunks + i])
+
+    def store(half):
+        at = pl.multiple_of((half * 2 + core) * cols, HD)
+        return pltpu.make_async_copy(
+            own.at[half], whole.at[:, pl.ds(at, cols)], sems.at[2 * chunks + half]
+        )
+
+    for half in range(2):
+        for i in range(chunks):
+            load(half, i).start()
+    for who in range(2):
+        for j in range(4):
+            at = pl.multiple_of(wrap(y + SHIFTS[j]) * wide, HD)
+            att[pl.ds(who * tok, tok), pl.ds(at, wide)] = att_refs[4 * who + j][...]
+    for half in range(2):
+        for i in range(chunks):
+            load(half, i).wait()
+            at = pl.ds(i * CHUNK, CHUNK)
+            got = jnp.dot(
+                att[...], held[pl.ds(half * rows, rows), at], preferred_element_type=jnp.float32
+            ).astype(own.dtype)
+            own[half, :, at] = got[:tok]
+            other_out[half, :, at] = got[tok:]
+        store(half).start()
+    for half in range(2):
+        store(half).wait()
+
+
+def project(own_att, other_att, weights):
     tok, wide = own_att[0].shape
     rows, cols = RING * wide, weights.shape[1]
-    piece = pl.BlockSpec((tok, wide), lambda i, *_: (0, 0))
+    vmem = pl.BlockSpec(memory_space=pltpu.VMEM)
+    anywhere = pl.BlockSpec(memory_space=pl.ANY)
     return pl.pallas_call(
-        functools.partial(project_kernel, base),
+        project_kernel,
         out_shape=[
             jax.ShapeDtypeStruct((tok, 4 * cols), jnp.bfloat16),
             jax.ShapeDtypeStruct((2, tok, cols), jnp.bfloat16),
         ],
-        grid_spec=pltpu.PrefetchScalarGridSpec(
-            num_scalar_prefetch=1,
-            grid=(2,),
-            in_specs=[piece] * 8 + [pl.BlockSpec((rows, cols), lambda i, *_: (i, 0))],
-            out_specs=[
-                pl.BlockSpec((tok, cols), lambda i, table: (0, i * 2 + table[base + 6])),
-                pl.BlockSpec((1, tok, cols), lambda i, *_: (i, 0, 0)),
-            ],
-            scratch_shapes=[pltpu.VMEM((2 * tok, rows), jnp.bfloat16)],
-        ),
+        in_specs=[vmem] * 8 + [anywhere],
+        out_specs=[anywhere, vmem],
+        scratch_shapes=[
+            pltpu.VMEM((2 * tok, rows), jnp.bfloat16),
+            pltpu.VMEM((2 * rows, cols), jnp.bfloat16),
+            pltpu.VMEM((2, tok, cols), jnp.bfloat16),
+            pltpu.SemaphoreType.DMA((2 * cols // CHUNK + 2,)),
+        ],
         compiler_params=pltpu.CompilerParams(vmem_limit_bytes=48 * 2**20),
         cost_estimate=pl.CostEstimate(
             flops=6 * 10**9, bytes_accessed=18 * 10**6, transcendentals=0
         ),
         name="project",
-    )(table, *own_att, *other_att, weights)
-
-
-def merge_kernel(base, table, theirs, whole, out, sems):
+    )(*own_att, *other_att, weights)
+
+
+def merge_kernel(theirs, whole, out, sems):
     del whole
     cols = theirs.shape[2]
+    core = lax.axis_index("c")
 
     def store(half):
-        at = pl.multiple_of((half * 2 + 1 - table[base + 6]) * cols, HD)
+        at = pl.multiple_of((half * 2 + 1 - core) * cols, HD)
         return pltpu.make_async_copy(theirs.at[half], out.at[:, pl.ds(at, cols)], sems.at[half])
 
     for half in range(2):
@@ -262,32 +284,27 @@
         store(half).wait()
 
 
-def merge(table, base, theirs, whole):
+def merge(theirs, whole):
     anywhere = pl.BlockSpec(memory_space=pl.ANY)
     return pl.pallas_call(
-        functools.partial(merge_kernel, base),
+        merge_kernel,
         out_shape=jax.ShapeDtypeStruct(whole.shape, whole.dtype),
-        in_specs=[
-            pl.BlockSpec(memory_space=pltpu.SMEM),
-            pl.BlockSpec(memory_space=pltpu.VMEM),
-            anywhere,
-        ],
+        in_specs=[pl.BlockSpec(memory_space=pltpu.VMEM), anywhere],
         out_specs=anywhere,
         scratch_shapes=[pltpu.SemaphoreType.DMA((2,))],
-        input_output_aliases={2: 0},
+        input_output_aliases={1: 0},
         cost_estimate=pl.CostEstimate(flops=0, bytes_accessed=3 * 10**6, transcendentals=0),
         name="merge",
-    )(table, theirs, whole)
+    )(theirs, whole)
 
 
 def per_device(query, keys, values, section_order, kept_sections, segment_ids, out_weight):
     tok = query.shape[1]
     sec = tok // 2
     nsec = section_order.shape[0]
-    zh, core = lax.axis_index("zh"), lax.axis_index("c")
     zl, x, y = lax.axis_index("zl"), lax.axis_index("x"), lax.axis_index("y")
     first, second = jnp.sum(segment_ids[0] < 1), jnp.sum(segment_ids[0] < 2)
-    scalars = jnp.stack([first, second, zl, x, y, zh * 2 + zl, core]).astype(jnp.int32)
+    scalars = jnp.stack([first, second, zl, x, y]).astype(jnp.int32)
     table = jnp.concatenate([section_order, kept_sections[0], scalars])
 
     def head_slice(array, shift):
@@ -316,9 +333,8 @@
         back[wrap_static(-shift)] = shifted(by_shift[shift], "y", shift)
     own_att = [back[s] for s in SHIFTS]
     other_att = [shifted(a, "c", 1, 2) for a in own_att]
-    base = 2 * nsec
-    whole, for_other = project(table, base, own_att, other_att, weights)
-    return merge(table, base, shifted(for_other, "c", 1, 2), whole)[None]
+    whole, for_other = project(own_att, other_att, weights)
+    return merge(shifted(for_other, "c", 1, 2), whole)[None]
 
 
 def wrap_static(shift):

time: 150 us -> 155 us (1.033); the launches traced: 150 us -> 152 us
  starting transfers between devices: 44.5 us -> 51 us
  Pallas kernels: 29.8 us -> 25 us
    all_gather x1, waiting for transfers between devices: 10.4 us -> 20.5 us  [per_device(): lax.all_gather(out_weight, ('zh', 'zl', 'x', 'y'), axis=0, tiled=True)]
    pallas_call x1, Pallas kernels: 16.8 us -> 7.04 us  [attention(): pl.pallas_call(functools.partial(attention_kernel, groups, sec, nsec, shi...]
    ppermute x22, waiting for transfers between devices: 39 us -> 29.6 us  [shifted(): lax.ppermute(array, axis, [(i, (i + step) % size) for i in range(size)])]
    ppermute x22, starting transfers between devices: 44.5 us -> 51 us  [shifted(): lax.ppermute(array, axis, [(i, (i + step) % size) for i in range(size)])]
    pallas_call x2, Pallas kernels: 13 us -> 18 us  [the longest x1 15.7 us: project(): pl.pallas_call(project_kernel, out_shape=[jax.ShapeDtypeStruct((tok, 4 *...]
    unnamed x18 -> x16, local copies, waits for them, and re-layouts: 4.35 us -> 4.35 us
  transfers between devices with their start and end apart: 23 -> 23, of which waited for: 10 -> 10; matrix products, arithmetic and copies ran while one was open for 5% -> 5% of each run, Pallas kernels for 11% -> 5%
where the time goes in v1:
time: 155 us; the launch traced here: 152 us
  starting transfers between devices  51 us (33%)
  waiting for transfers between devices  50.7 us (33%)
  Pallas kernels  25 us (16%)
  between operations  13.5 us (9%)
  local copies, waits for them, and re-layouts  10.3 us (7%)
  other arithmetic  1.64 us (1%)
    ppermute x22, starting transfers between devices, shifted(): lax.ppermute(array, axis, [(i, (i + step) % size) for i in range(size)])  51 us
    ppermute x22, waiting for transfers between devices, shifted(): lax.ppermute(array, axis, [(i, (i + step) % size) for i in range(size)])  29.6 us
    all_gather x1, waiting for transfers between devices, per_device(): lax.all_gather(out_weight, ('zh', 'zl', 'x', 'y'), axis=0, tiled=True)  20.5 us
    pallas_call x1, Pallas kernels, project(): pl.pallas_call(project_kernel, out_shape=[jax.ShapeDtypeStruct((tok, 4 *...  15.7 us
    pallas_call x1, Pallas kernels, attention(): pl.pallas_call(functools.partial(attention_kernel, groups, sec, nsec, shi...  7.04 us
    unnamed x16, local copies, waits for them, and re-layouts  4.35 us
    dynamic_slice x2, local copies, waits for them, and re-layouts, head_slice(): return lax.dynamic_slice_in_dim(array[0], wrap(y + shift) * wide, wide, 1)  3.25 us
  transfers between devices with their start and end apart: 23, of which 10 were waited for; matrix products, arithmetic and copies ran while one was open for 5% of the time, Pallas kernels for 5%

profile of v1, /device:TPU:1, one launch (start us, length us, event | category | flops | bytes accessed | tf_op | source)
XLA Modules:
  0.0 152.2 jit_solution(5475443448992964148)
XLA Ops:
  8.4 2.2 %collective-permute-start.3 = (bf16[224,256]{1,0:T(8,128)(2,1)S(1)}, bf16[224,256]{1,0:T(8,128)(2,1)S(1)}, u32[]{:S(2)}, u32[]{:S(2)}) collective-permute-start(bf16[224,256]{1,0:T(8,128)(2,1)S(1)} %pad_maximum_fusion.2), channel_id=1, source_target_pairs={{0,1},{1,2},{2,3},{3,0},{4,5},{5,6},{6,7},{7,4},{8,9},{9,10},{10,1... | collective-permute-start | bytes 344072 | tf_op jit(solution)/shard_map/ppermute | solution.py:21
  10.6 1.5 %collective-permute-start.4 = (bf16[224,256]{1,0:T(8,128)(2,1)S(1)}, bf16[224,256]{1,0:T(8,128)(2,1)S(1)}, u32[]{:S(2)}, u32[]{:S(2)}) collective-permute-start(bf16[224,256]{1,0:T(8,128)(2,1)S(1)} %pad_maximum_fusion.3), channel_id=1, source_target_pairs={{0,3},{1,0},{2,1},{3,2},{4,7},{5,4},{6,5},{7,6},{8,11},{9,8},{10,9... | collective-permute-start | bytes 344072 | tf_op jit(solution)/shard_map/ppermute | solution.py:21
  12.1 1.7 %collective-permute-start.5 = (bf16[224,256]{1,0:T(8,128)(2,1)S(1)}, bf16[224,256]{1,0:T(8,128)(2,1)S(1)}, u32[]{:S(2)}, u32[]{:S(2)}) collective-permute-start(bf16[224,256]{1,0:T(8,128)(2,1)S(1)} %pad_maximum_fusion.4), channel_id=1, source_target_pairs={{0,2},{1,3},{2,0},{3,1},{4,6},{5,7},{6,4},{7,5},{8,10},{9,11},{10,... | collective-permute-start | bytes 344072 | tf_op jit(solution)/shard_map/ppermute | solution.py:21
  14.7 3.5 %collective-permute-done.5 = bf16[224,256]{1,0:T(8,128)(2,1)S(1)} collective-permute-done((bf16[224,256]{1,0:T(8,128)(2,1)S(1)}, bf16[224,256]{1,0:T(8,128)(2,1)S(1)}, u32[]{:S(2)}, u32[]{:S(2)}) %collective-permute-start.5) | collective-permute-done | bytes 114720 | tf_op jit(solution)/shard_map/ppermute | solution.py:21
  19.5 1.5 %collective-permute-start.7 = (bf16[4,224,256]{2,1,0:T(8,128)(2,1)S(1)}, bf16[4,224,256]{2,1,0:T(8,128)(2,1)S(1)}, u32[]{:S(2)}, u32[]{:S(2)}) collective-permute-start(bf16[4,224,256]{2,1,0:T(8,128)(2,1)S(1)} %pad_maximum_fusion.refs_4_), channel_id=1, source_target_pairs={{0,12},{4,0},{8,4},{12,8},{1,13},{5,1},{9,5},{13,9},{2,14},{6,2},{... | collective-permute-start | bytes 1376264 | tf_op jit(solution)/shard_map/ppermute | solution.py:21
  21.0 1.6 %collective-permute-start.10 = (bf16[4,224,256]{2,1,0:T(8,128)(2,1)S(1)}, bf16[4,224,256]{2,1,0:T(8,128)(2,1)S(1)}, u32[]{:S(2)}, u32[]{:S(2)}) collective-permute-start(bf16[4,224,256]{2,1,0:T(8,128)(2,1)S(1)} %pad_maximum_fusion.refs_4_), channel_id=1, source_target_pairs={{0,16},{16,0},{1,17},{17,1},{2,18},{18,2},{3,19},{19,3},{4,20},{20... | collective-permute-start | bytes 1376264 | tf_op jit(solution)/shard_map/ppermute | solution.py:21
  22.6 8.2 %collective-permute-done.6.refs_5_ = bf16[4,224,256]{2,1,0:T(8,128)(2,1)S(1)} collective-permute-done((bf16[4,224,256]{2,1,0:T(8,128)(2,1)S(1)}, bf16[4,224,256]{2,1,0:T(8,128)(2,1)S(1)}, u32[]{:S(2)}, u32[]{:S(2)}) %collective-permute-start.6) | collective-permute-done | bytes 458784 | tf_op jit(solution)/shard_map/ppermute | solution.py:21
  32.2 2.7 %collective-permute-start.9 = (bf16[2,224,256]{2,1,0:T(8,128)(2,1)}, bf16[2,224,256]{2,1,0:T(8,128)(2,1)S(1)}, u32[]{:S(2)}, u32[]{:S(2)}) collective-permute-start(bf16[2,224,256]{2,1,0:T(8,128)(2,1)} %slice.9), channel_id=1, source_target_pairs={{0,12},{4,0},{8,4},{12,8},{1,13},{5,1},{9,5},{13,9},{2,14},{6,2},{... | collective-permute-start | bytes 688136 | tf_op jit(solution)/shard_map/ppermute | solution.py:21
  34.9 2.2 %dynamic-slice_bitcast_fusion = (bf16[224,640]{1,0:T(8,128)(2,1)}, bf16[224,640]{1,0:T(8,128)(2,1)S(1)}, bf16[224,640]{1,0:T(8,128)(2,1)S(1)}, bf16[224,640]{1,0:T(8,128)(2,1)}) fusion(bf16[1,224,2560]{2,1,0:T(8,128)(2,1)} %param.7, s32[]{:T(128)S(6)} %select_n.31, s32[]{:T(128)S(6)} %select_n.29, s32[]{:T(128)S(6)} %select_n.28, s32[]{:T(128)S(6)} %select_n.30), kind=kLoop, calls=%fused_computation.2 | loop fusion | bytes 2293776 | tf_op jit(solution)/shard_map/dynamic_slice | solution.py:312
  37.2 2.7 %collective-permute-start.12 = (bf16[4,224,256]{2,1,0:T(8,128)(2,1)S(1)}, bf16[4,224,256]{2,1,0:T(8,128)(2,1)S(1)}, u32[]{:S(2)}, u32[]{:S(2)}) collective-permute-start(bf16[4,224,256]{2,1,0:T(8,128)(2,1)S(1)} %collective-permute-done.10.refs_9_), channel_id=1, source_target_pairs={{0,12},{4,0},{8,4},{12,8},{1,13},{5,1},{9,5},{13,9},{2,14},{6,2},{... | collective-permute-start | bytes 1376264 | tf_op jit(solution)/shard_map/ppermute | solution.py:21
  40.7 1.5 %collective-permute-start.13 = (bf16[4,224,256]{2,1,0:T(8,128)(2,1)}, bf16[4,224,256]{2,1,0:T(8,128)(2,1)}, u32[]{:S(2)}, u32[]{:S(2)}) collective-permute-start(bf16[4,224,256]{2,1,0:T(8,128)(2,1)} %pad_maximum_fusion.1), channel_id=1, source_target_pairs={{0,16},{16,0},{1,17},{17,1},{2,18},{18,2},{3,19},{19,3},{4,20},{20... | collective-permute-start | bytes 1376264 | tf_op jit(solution)/shard_map/ppermute | solution.py:21
  42.2 2.6 %collective-permute-start.1 = (bf16[224,640]{1,0:T(8,128)(2,1)}, bf16[224,640]{1,0:T(8,128)(2,1)}, u32[]{:S(2)}, u32[]{:S(2)}) collective-permute-start(bf16[224,640]{1,0:T(8,128)(2,1)} %get-tuple-element.22), channel_id=1, source_target_pairs={{0,3},{1,0},{2,1},{3,2},{4,7},{5,4},{6,5},{7,6},{8,11},{9,8},{10,9... | collective-permute-start | bytes 860168 | tf_op jit(solution)/shard_map/ppermute | solution.py:21
  46.2 1.3 concatenate.18.table
  47.5 7.8 %collective-permute-done.1.refs_2_ = bf16[224,640]{1,0:T(8,128)(2,1)} collective-permute-done((bf16[224,640]{1,0:T(8,128)(2,1)}, bf16[224,640]{1,0:T(8,128)(2,1)}, u32[]{:S(2)}, u32[]{:S(2)}) %collective-permute-start.1) | collective-permute-done | bytes 286752 | tf_op jit(solution)/shard_map/ppermute | solution.py:21
  55.3 4.1 %collective-permute-done.2.refs_3_ = bf16[224,640]{1,0:T(8,128)(2,1)} collective-permute-done((bf16[224,640]{1,0:T(8,128)(2,1)}, bf16[224,640]{1,0:T(8,128)(2,1)}, u32[]{:S(2)}, u32[]{:S(2)}) %collective-permute-start.2) | collective-permute-done | bytes 286752 | tf_op jit(solution)/shard_map/ppermute | solution.py:21
  60.3 7.0 %attend.1 = (bf16[224,640]{1,0:T(8,128)(2,1)S(1)}, bf16[224,640]{1,0:T(8,128)(2,1)S(1)}, bf16[224,640]{1,0:T(8,128)(2,1)S(1)}, bf16[224,640]{1,0:T(8,128)(2,1)S(1)}) custom-call(s32[133]{0:T(256)S(1)} %concatenate.18.table, bf16[224,640]{1,0:T(8,128)(2,1)S(1)} %get-tuple-element.21.refs_0_, bf16[224,640]{1,0:T(8,128)(2,1)S(1)} %copy-done.1, ...), custom_call_target="tpu_custom_call" | custom-call | flops 8000000000 | bytes 6000000 | tf_op jit(solution)/shard_map/attend/pallas_call | solution.py:182
  67.4 4.7 %collective-permute-start.14 = (bf16[224,640]{1,0:T(8,128)(2,1)S(1)}, bf16[224,640]{1,0:T(8,128)(2,1)S(1)}, u32[]{:S(2)}, u32[]{:S(2)}) collective-permute-start(bf16[224,640]{1,0:T(8,128)(2,1)S(1)} %get-tuple-element.12), channel_id=1, source_target_pairs={{0,1},{1,2},{2,3},{3,0},{4,5},{5,6},{6,7},{7,4},{8,9},{9,10},{10,1... | collective-permute-start | bytes 860168 | tf_op jit(solution)/shard_map/ppermute | solution.py:21
  74.1 3.9 %collective-permute-start.17 = (bf16[224,640]{1,0:T(8,128)(2,1)S(1)}, bf16[224,640]{1,0:T(8,128)(2,1)S(1)}, u32[]{:S(2)}, u32[]{:S(2)}) collective-permute-start(bf16[224,640]{1,0:T(8,128)(2,1)S(1)} %get-tuple-element.11.refs_0_), channel_id=1, source_target_pairs={{0,32},{32,0},{1,33},{33,1},{2,34},{34,2},{3,35},{35,3},{4,36},{36... | collective-permute-start | bytes 860168 | tf_op jit(solution)/shard_map/ppermute | solution.py:21
  79.3 10.3 %collective-permute-start.18 = (bf16[224,640]{1,0:T(8,128)(2,1)S(1)}, bf16[224,640]{1,0:T(8,128)(2,1)S(1)}, u32[]{:S(2)}, u32[]{:S(2)}) collective-permute-start(bf16[224,640]{1,0:T(8,128)(2,1)S(1)} %collective-permute-done.14.refs_1_), channel_id=1, source_target_pairs={{0,32},{32,0},{1,33},{33,1},{2,34},{34,2},{3,35},{35,3},{4,36},{36... | collective-permute-start | bytes 860168 | tf_op jit(solution)/shard_map/ppermute | solution.py:21
  91.6 9.1 %collective-permute-start.20 = (bf16[224,640]{1,0:T(8,128)(2,1)S(1)}, bf16[224,640]{1,0:T(8,128)(2,1)S(1)}, u32[]{:S(2)}, u32[]{:S(2)}) collective-permute-start(bf16[224,640]{1,0:T(8,128)(2,1)S(1)} %collective-permute-done.16.refs_3_), channel_id=1, source_target_pairs={{0,32},{32,0},{1,33},{33,1},{2,34},{34,2},{3,35},{35,3},{4,36},{36... | collective-permute-start | bytes 860168 | tf_op jit(solution)/shard_map/ppermute | solution.py:21
  101.9 20.5 %all-gather.2.cloned.1.call-done.refs_8_ = bf16[5120,1280]{1,0:T(8,128)(2,1)} async-done(((bf16[80,1280]{1,0:T(8,128)(2,1)}), bf16[5120,1280]{1,0:T(8,128)(2,1)}) %all-gather.2.cloned.1.call-update) | async-done | bytes 13107216 | tf_op jit(solution)/shard_map/all_gather | solution.py:314
  123.4 15.7 %project.1 = (bf16[224,5120]{1,0:T(8,128)(2,1)}, bf16[2,224,1280]{2,1,0:T(8,128)(2,1)S(1)}) custom-call(bf16[224,640]{1,0:T(8,128)(2,1)S(1)} %copy-done.3, bf16[224,640]{1,0:T(8,128)(2,1)S(1)} %collective-permute-done.14.refs_1_, bf16[224,640]{1,0:T(8,128)(2,1)S(1)} %collective-permute-done.15.refs_2_, bf16[224,640]{1,0:T(8,128)(2,1)S(1)} %collective-permute-done.16.refs_3_, ...), custom_call_target="tpu_custom_call" | custom-call | flops 6000000000 | bytes 18000000 | tf_op jit(solution)/shard_map/project/pallas_call | solution.py:250
  139.6 2.4 %collective-permute-done.21.theirs = bf16[2,224,1280]{2,1,0:T(8,128)(2,1)S(1)} collective-permute-done((bf16[2,224,1280]{2,1,0:T(8,128)(2,1)S(1)}, bf16[2,224,1280]{2,1,0:T(8,128)(2,1)S(1)}, u32[]{:S(2)}, u32[]{:S(2)}) %collective-permute-start.21) | collective-permute-done | bytes 1146912 | tf_op jit(solution)/shard_map/ppermute | solution.py:21
  143.0 2.3 %merge.1 = bf16[224,5120]{1,0:T(8,128)(2,1)} custom-call(bf16[2,224,1280]{2,1,0:T(8,128)(2,1)} %copy-done.4, bf16[224,5120]{1,0:T(8,128)(2,1)} %get-tuple-element.16.whole), custom_call_target="tpu_custom_call", output_to_operand_aliasing={{}: (1, {})} | custom-call | bytes 3000000 | tf_op jit(solution)/shard_map/merge/pallas_call | solution.py:289
  (54 shorter events, 17.7 us)
Async XLA Ops:
  6.5 115.9 %all-gather.2.cloned.1.call-start = ((), (), s32[]{:S(2)}) async-start(), calls=%async_computation | async-start | bytes 13312000 | tf_op jit(solution)/shard_map/all_gather | solution.py:314
  8.4 6.4 %collective-permute-start.3 = (bf16[224,256]{1,0:T(8,128)(2,1)S(1)}, bf16[224,256]{1,0:T(8,128)(2,1)S(1)}, u32[]{:S(2)}, u32[]{:S(2)}) collective-permute-start(bf16[224,256]{1,0:T(8,128)(2,1)S(1)} %pad_maximum_fusion.2), channel_id=1, source_target_pairs={{0,1},{1,2},{2,3},{3,0},{4,5},{5,6},{6,7},{7,4},{8,9},{9,10},{10,1... | collective-permute-start | bytes 344072 | tf_op jit(solution)/shard_map/ppermute | solution.py:21
  10.6 4.1 %collective-permute-start.4 = (bf16[224,256]{1,0:T(8,128)(2,1)S(1)}, bf16[224,256]{1,0:T(8,128)(2,1)S(1)}, u32[]{:S(2)}, u32[]{:S(2)}) collective-permute-start(bf16[224,256]{1,0:T(8,128)(2,1)S(1)} %pad_maximum_fusion.3), channel_id=1, source_target_pairs={{0,3},{1,0},{2,1},{3,2},{4,7},{5,4},{6,5},{7,6},{8,11},{9,8},{10,9... | collective-permute-start | bytes 344072 | tf_op jit(solution)/shard_map/ppermute | solution.py:21
  12.1 6.1 %collective-permute-start.5 = (bf16[224,256]{1,0:T(8,128)(2,1)S(1)}, bf16[224,256]{1,0:T(8,128)(2,1)S(1)}, u32[]{:S(2)}, u32[]{:S(2)}) collective-permute-start(bf16[224,256]{1,0:T(8,128)(2,1)S(1)} %pad_maximum_fusion.4), channel_id=1, source_target_pairs={{0,2},{1,3},{2,0},{3,1},{4,6},{5,7},{6,4},{7,5},{8,10},{9,11},{10,... | collective-permute-start | bytes 344072 | tf_op jit(solution)/shard_map/ppermute | solution.py:21
  18.3 12.5 %collective-permute-start.6 = (bf16[4,224,256]{2,1,0:T(8,128)(2,1)S(1)}, bf16[4,224,256]{2,1,0:T(8,128)(2,1)S(1)}, u32[]{:S(2)}, u32[]{:S(2)}) collective-permute-start(bf16[4,224,256]{2,1,0:T(8,128)(2,1)S(1)} %pad_maximum_fusion.refs_4_), channel_id=1, source_target_pairs={{0,4},{4,8},{8,12},{12,0},{1,5},{5,9},{9,13},{13,1},{2,6},{6,10},{... | collective-permute-start | bytes 1376264 | tf_op jit(solution)/shard_map/ppermute | solution.py:21
  19.5 12.0 %collective-permute-start.7 = (bf16[4,224,256]{2,1,0:T(8,128)(2,1)S(1)}, bf16[4,224,256]{2,1,0:T(8,128)(2,1)S(1)}, u32[]{:S(2)}, u32[]{:S(2)}) collective-permute-start(bf16[4,224,256]{2,1,0:T(8,128)(2,1)S(1)} %pad_maximum_fusion.refs_4_), channel_id=1, source_target_pairs={{0,12},{4,0},{8,4},{12,8},{1,13},{5,1},{9,5},{13,9},{2,14},{6,2},{... | collective-permute-start | bytes 1376264 | tf_op jit(solution)/shard_map/ppermute | solution.py:21
  21.0 16.1 %collective-permute-start.10 = (bf16[4,224,256]{2,1,0:T(8,128)(2,1)S(1)}, bf16[4,224,256]{2,1,0:T(8,128)(2,1)S(1)}, u32[]{:S(2)}, u32[]{:S(2)}) collective-permute-start(bf16[4,224,256]{2,1,0:T(8,128)(2,1)S(1)} %pad_maximum_fusion.refs_4_), channel_id=1, source_target_pairs={{0,16},{16,0},{1,17},{17,1},{2,18},{18,2},{3,19},{19,3},{4,20},{20... | collective-permute-start | bytes 1376264 | tf_op jit(solution)/shard_map/ppermute | solution.py:21
  31.5 8.3 %collective-permute-start.8 = (bf16[2,224,256]{2,1,0:T(8,128)(2,1)}, bf16[2,224,256]{2,1,0:T(8,128)(2,1)S(1)}, u32[]{:S(2)}, u32[]{:S(2)}) collective-permute-start(bf16[2,224,256]{2,1,0:T(8,128)(2,1)} %slice.8), channel_id=1, source_target_pairs={{0,4},{4,8},{8,12},{12,0},{1,5},{5,9},{9,13},{13,1},{2,6},{6,10},{... | collective-permute-start | bytes 688136 | tf_op jit(solution)/shard_map/ppermute | solution.py:21
  32.2 7.6 %collective-permute-start.9 = (bf16[2,224,256]{2,1,0:T(8,128)(2,1)}, bf16[2,224,256]{2,1,0:T(8,128)(2,1)S(1)}, u32[]{:S(2)}, u32[]{:S(2)}) collective-permute-start(bf16[2,224,256]{2,1,0:T(8,128)(2,1)} %slice.9), channel_id=1, source_target_pairs={{0,12},{4,0},{8,4},{12,8},{1,13},{5,1},{9,5},{13,9},{2,14},{6,2},{... | collective-permute-start | bytes 688136 | tf_op jit(solution)/shard_map/ppermute | solution.py:21
  34.9 11.3 %copy-start.7 = (s32[1,64]{1,0:T(1,128)S(1)}, s32[1,64]{1,0:T(1,128)}, u32[]{:S(2)}) copy-start(s32[1,64]{1,0:T(1,128)} %param.11) | copy-start | bytes 772
  37.1 7.7 %collective-permute-start = (bf16[224,640]{1,0:T(8,128)(2,1)S(1)}, bf16[224,640]{1,0:T(8,128)(2,1)S(1)}, u32[]{:S(2)}, u32[]{:S(2)}) collective-permute-start(bf16[224,640]{1,0:T(8,128)(2,1)S(1)} %get-tuple-element.20), channel_id=1, source_target_pairs={{0,1},{1,2},{2,3},{3,0},{4,5},{5,6},{6,7},{7,4},{8,9},{9,10},{10,1... | collective-permute-start | bytes 860168 | tf_op jit(solution)/shard_map/ppermute | solution.py:21
  37.1 22.3 %collective-permute-start.11 = (bf16[4,224,256]{2,1,0:T(8,128)(2,1)S(1)}, bf16[4,224,256]{2,1,0:T(8,128)(2,1)S(1)}, u32[]{:S(2)}, u32[]{:S(2)}) collective-permute-start(bf16[4,224,256]{2,1,0:T(8,128)(2,1)S(1)} %collective-permute-done.10.refs_9_), channel_id=1, source_target_pairs={{0,4},{4,8},{8,12},{12,0},{1,5},{5,9},{9,13},{13,1},{2,6},{6,10},{... | collective-permute-start | bytes 1376264 | tf_op jit(solution)/shard_map/ppermute | solution.py:21
  37.2 22.2 %collective-permute-start.12 = (bf16[4,224,256]{2,1,0:T(8,128)(2,1)S(1)}, bf16[4,224,256]{2,1,0:T(8,128)(2,1)S(1)}, u32[]{:S(2)}, u32[]{:S(2)}) collective-permute-start(bf16[4,224,256]{2,1,0:T(8,128)(2,1)S(1)} %collective-permute-done.10.refs_9_), channel_id=1, source_target_pairs={{0,12},{4,0},{8,4},{12,8},{1,13},{5,1},{9,5},{13,9},{2,14},{6,2},{... | collective-permute-start | bytes 1376264 | tf_op jit(solution)/shard_map/ppermute | solution.py:21
  40.7 18.7 %collective-permute-start.13 = (bf16[4,224,256]{2,1,0:T(8,128)(2,1)}, bf16[4,224,256]{2,1,0:T(8,128)(2,1)}, u32[]{:S(2)}, u32[]{:S(2)}) collective-permute-start(bf16[4,224,256]{2,1,0:T(8,128)(2,1)} %pad_maximum_fusion.1), channel_id=1, source_target_pairs={{0,16},{16,0},{1,17},{17,1},{2,18},{18,2},{3,19},{19,3},{4,20},{20... | collective-permute-start | bytes 1376264 | tf_op jit(solution)/shard_map/ppermute | solution.py:21
  42.2 13.1 %collective-permute-start.1 = (bf16[224,640]{1,0:T(8,128)(2,1)}, bf16[224,640]{1,0:T(8,128)(2,1)}, u32[]{:S(2)}, u32[]{:S(2)}) collective-permute-start(bf16[224,640]{1,0:T(8,128)(2,1)} %get-tuple-element.22), channel_id=1, source_target_pairs={{0,3},{1,0},{2,1},{3,2},{4,7},{5,4},{6,5},{7,6},{8,11},{9,8},{10,9... | collective-permute-start | bytes 860168 | tf_op jit(solution)/shard_map/ppermute | solution.py:21
  45.5 13.9 %collective-permute-start.2 = (bf16[224,640]{1,0:T(8,128)(2,1)}, bf16[224,640]{1,0:T(8,128)(2,1)}, u32[]{:S(2)}, u32[]{:S(2)}) collective-permute-start(bf16[224,640]{1,0:T(8,128)(2,1)} %get-tuple-element.19), channel_id=1, source_target_pairs={{0,2},{1,3},{2,0},{3,1},{4,6},{5,7},{6,4},{7,5},{8,10},{9,11},{10,... | collective-permute-start | bytes 860168 | tf_op jit(solution)/shard_map/ppermute | solution.py:21
  67.4 11.9 %collective-permute-start.14 = (bf16[224,640]{1,0:T(8,128)(2,1)S(1)}, bf16[224,640]{1,0:T(8,128)(2,1)S(1)}, u32[]{:S(2)}, u32[]{:S(2)}) collective-permute-start(bf16[224,640]{1,0:T(8,128)(2,1)S(1)} %get-tuple-element.12), channel_id=1, source_target_pairs={{0,1},{1,2},{2,3},{3,0},{4,5},{5,6},{6,7},{7,4},{8,9},{9,10},{10,1... | collective-permute-start | bytes 860168 | tf_op jit(solution)/shard_map/ppermute | solution.py:21
  72.1 17.6 %collective-permute-start.15 = (bf16[224,640]{1,0:T(8,128)(2,1)S(1)}, bf16[224,640]{1,0:T(8,128)(2,1)S(1)}, u32[]{:S(2)}, u32[]{:S(2)}) collective-permute-start(bf16[224,640]{1,0:T(8,128)(2,1)S(1)} %get-tuple-element.13), channel_id=1, source_target_pairs={{0,3},{1,0},{2,1},{3,2},{4,7},{5,4},{6,5},{7,6},{8,11},{9,8},{10,9... | collective-permute-start | bytes 860168 | tf_op jit(solution)/shard_map/ppermute | solution.py:21
  73.0 18.6 %collective-permute-start.16 = (bf16[224,640]{1,0:T(8,128)(2,1)S(1)}, bf16[224,640]{1,0:T(8,128)(2,1)S(1)}, u32[]{:S(2)}, u32[]{:S(2)}) collective-permute-start(bf16[224,640]{1,0:T(8,128)(2,1)S(1)} %get-tuple-element.14), channel_id=1, source_target_pairs={{0,2},{1,3},{2,0},{3,1},{4,6},{5,7},{6,4},{7,5},{8,10},{9,11},{10,... | collective-permute-start | bytes 860168 | tf_op jit(solution)/shard_map/ppermute | solution.py:21
  74.1 26.7 %collective-permute-start.17 = (bf16[224,640]{1,0:T(8,128)(2,1)S(1)}, bf16[224,640]{1,0:T(8,128)(2,1)S(1)}, u32[]{:S(2)}, u32[]{:S(2)}) collective-permute-start(bf16[224,640]{1,0:T(8,128)(2,1)S(1)} %get-tuple-element.11.refs_0_), channel_id=1, source_target_pairs={{0,32},{32,0},{1,33},{33,1},{2,34},{34,2},{3,35},{35,3},{4,36},{36... | collective-permute-start | bytes 860168 | tf_op jit(solution)/shard_map/ppermute | solution.py:21
  79.3 21.4 %collective-permute-start.18 = (bf16[224,640]{1,0:T(8,128)(2,1)S(1)}, bf16[224,640]{1,0:T(8,128)(2,1)S(1)}, u32[]{:S(2)}, u32[]{:S(2)}) collective-permute-start(bf16[224,640]{1,0:T(8,128)(2,1)S(1)} %collective-permute-done.14.refs_1_), channel_id=1, source_target_pairs={{0,32},{32,0},{1,33},{33,1},{2,34},{34,2},{3,35},{35,3},{4,36},{36... | collective-permute-start | bytes 860168 | tf_op jit(solution)/shard_map/ppermute | solution.py:21
  89.7 11.1 %collective-permute-start.19 = (bf16[224,640]{1,0:T(8,128)(2,1)S(1)}, bf16[224,640]{1,0:T(8,128)(2,1)S(1)}, u32[]{:S(2)}, u32[]{:S(2)}) collective-permute-start(bf16[224,640]{1,0:T(8,128)(2,1)S(1)} %collective-permute-done.15.refs_2_), channel_id=1, source_target_pairs={{0,32},{32,0},{1,33},{33,1},{2,34},{34,2},{3,35},{35,3},{4,36},{36... | collective-permute-start | bytes 860168 | tf_op jit(solution)/shard_map/ppermute | solution.py:21
  91.6 10.3 %collective-permute-start.20 = (bf16[224,640]{1,0:T(8,128)(2,1)S(1)}, bf16[224,640]{1,0:T(8,128)(2,1)S(1)}, u32[]{:S(2)}, u32[]{:S(2)}) collective-permute-start(bf16[224,640]{1,0:T(8,128)(2,1)S(1)} %collective-permute-done.16.refs_3_), channel_id=1, source_target_pairs={{0,32},{32,0},{1,33},{33,1},{2,34},{34,2},{3,35},{35,3},{4,36},{36... | collective-permute-start | bytes 860168 | tf_op jit(solution)/shard_map/ppermute | solution.py:21
  139.1 3.0 %collective-permute-start.21 = (bf16[2,224,1280]{2,1,0:T(8,128)(2,1)S(1)}, bf16[2,224,1280]{2,1,0:T(8,128)(2,1)S(1)}, u32[]{:S(2)}, u32[]{:S(2)}) collective-permute-start(bf16[2,224,1280]{2,1,0:T(8,128)(2,1)S(1)} %get-tuple-element.15), channel_id=1, source_target_pairs={{0,32},{32,0},{1,33},{33,1},{2,34},{34,2},{3,35},{35,3},{4,36},{36... | collective-permute-start | bytes 3440648 | tf_op jit(solution)/shard_map/ppermute | solution.py:21
  (7 other events, 26.3 us)
Sparse Core Ops, SparseCore 0:
  10.2 112.1 all-gather.1

commit v2 on v0

--- a/solution.py
+++ b/solution.py
@@ -191,7 +191,7 @@
             pltpu.VMEM((groups * sec, HD), jnp.float32),
             pltpu.SemaphoreType.DMA,
         ],
-        compiler_params=pltpu.CompilerParams(vmem_limit_bytes=48 * 2**20),
+        compiler_params=pltpu.CompilerParams(vmem_limit_bytes=24 * 2**20),
         cost_estimate=pl.CostEstimate(
             flops=count * 2 * 10**9,
             bytes_accessed=6 * 10**6,
@@ -240,7 +240,7 @@
             ],
             scratch_shapes=[pltpu.VMEM((2 * tok, rows), jnp.bfloat16)],
         ),
-        compiler_params=pltpu.CompilerParams(vmem_limit_bytes=48 * 2**20),
+        compiler_params=pltpu.CompilerParams(vmem_limit_bytes=32 * 2**20),
         cost_estimate=pl.CostEstimate(
             flops=6 * 10**9, bytes_accessed=18 * 10**6, transcendentals=0
         ),
@@ -275,6 +275,7 @@
         out_specs=anywhere,
         scratch_shapes=[pltpu.SemaphoreType.DMA((2,))],
         input_output_aliases={2: 0},
+        compiler_params=pltpu.CompilerParams(vmem_limit_bytes=8 * 2**20),
         cost_estimate=pl.CostEstimate(flops=0, bytes_accessed=3 * 10**6, transcendentals=0),
         name="merge",
     )(table, theirs, whole)

time: 150 us -> 150 us (level)
  starting transfers between devices: 44.5 us -> 60.6 us
  waiting for transfers between devices: 50.2 us -> 36.9 us
  Pallas kernels: 29.8 us -> 23.4 us
  local copies, waits for them, and re-layouts: 10.3 us -> 14 us
    ppermute x22, starting transfers between devices: 44.5 us -> 60.6 us  [shifted(): lax.ppermute(array, axis, [(i, (i + step) % size) for i in range(size)])]
    ppermute x22, waiting for transfers between devices: 39 us -> 28.1 us  [shifted(): lax.ppermute(array, axis, [(i, (i + step) % size) for i in range(size)])]
    unnamed x18 -> x16, local copies, waits for them, and re-layouts: 4.35 us -> 8.06 us
    pallas_call x1, Pallas kernels: 10.7 us -> 7.84 us  [project(): pl.pallas_call(functools.partial(project_kernel, base), out_shape=[jax.Sh...]
    pallas_call x1, Pallas kernels: 16.8 us -> 14 us  [attention(): pl.pallas_call(functools.partial(attention_kernel, groups, sec, nsec, shi...]
    all_gather x1, waiting for transfers between devices: 10.4 us -> 8.07 us  [per_device(): lax.all_gather(out_weight, ('zh', 'zl', 'x', 'y'), axis=0, tiled=True)]
  transfers between devices with their start and end apart: 23 -> 23, of which waited for: 10 -> 8; matrix products, arithmetic and copies ran while one was open for 5% -> 5% of each run, Pallas kernels for 11% -> 9%
where the time goes in v2:
time: 150 us
  starting transfers between devices  60.6 us (40%)
  waiting for transfers between devices  36.9 us (25%)
  Pallas kernels  23.4 us (16%)
  local copies, waits for them, and re-layouts  14 us (9%)
  between operations  13.5 us (9%)
  other arithmetic  1.64 us (1%)
    ppermute x22, starting transfers between devices, shifted(): lax.ppermute(array, axis, [(i, (i + step) % size) for i in range(size)])  60.6 us
    ppermute x22, waiting for transfers between devices, shifted(): lax.ppermute(array, axis, [(i, (i + step) % size) for i in range(size)])  28.1 us
    pallas_call x1, Pallas kernels, attention(): pl.pallas_call(functools.partial(attention_kernel, groups, sec, nsec, shi...  14 us
    all_gather x1, waiting for transfers between devices, per_device(): lax.all_gather(out_weight, ('zh', 'zl', 'x', 'y'), axis=0, tiled=True)  8.07 us
    unnamed x16, local copies, waits for them, and re-layouts  8.06 us
    pallas_call x1, Pallas kernels, project(): pl.pallas_call(functools.partial(project_kernel, base), out_shape=[jax.Sh...  7.84 us
    dynamic_slice x2, local copies, waits for them, and re-layouts, head_slice(): return lax.dynamic_slice_in_dim(array[0], wrap(y + shift) * wide, wide, 1)  3.25 us
  transfers between devices with their start and end apart: 23, of which 8 were waited for; matrix products, arithmetic and copies ran while one was open for 5% of the time, Pallas kernels for 9%

profile of v2, /device:TPU:1, one launch (start us, length us, event | category | flops | bytes accessed | tf_op | source)
XLA Modules:
  0.0 150.1 jit_solution(10463302879269799295)
XLA Ops:
  8.4 2.2 %collective-permute-start.3 = (bf16[224,256]{1,0:T(8,128)(2,1)S(1)}, bf16[224,256]{1,0:T(8,128)(2,1)S(1)}, u32[]{:S(2)}, u32[]{:S(2)}) collective-permute-start(bf16[224,256]{1,0:T(8,128)(2,1)S(1)} %pad_maximum_fusion.2), channel_id=1, source_target_pairs={{0,1},{1,2},{2,3},{3,0},{4,5},{5,6},{6,7},{7,4},{8,9},{9,10},{10,1... | collective-permute-start | bytes 344072 | tf_op jit(solution)/shard_map/ppermute | solution.py:20
  10.6 1.5 %collective-permute-start.4 = (bf16[224,256]{1,0:T(8,128)(2,1)S(1)}, bf16[224,256]{1,0:T(8,128)(2,1)S(1)}, u32[]{:S(2)}, u32[]{:S(2)}) collective-permute-start(bf16[224,256]{1,0:T(8,128)(2,1)S(1)} %pad_maximum_fusion.3), channel_id=1, source_target_pairs={{0,3},{1,0},{2,1},{3,2},{4,7},{5,4},{6,5},{7,6},{8,11},{9,8},{10,9... | collective-permute-start | bytes 344072 | tf_op jit(solution)/shard_map/ppermute | solution.py:20
  12.1 1.7 %collective-permute-start.5 = (bf16[224,256]{1,0:T(8,128)(2,1)S(1)}, bf16[224,256]{1,0:T(8,128)(2,1)S(1)}, u32[]{:S(2)}, u32[]{:S(2)}) collective-permute-start(bf16[224,256]{1,0:T(8,128)(2,1)S(1)} %pad_maximum_fusion.4), channel_id=1, source_target_pairs={{0,2},{1,3},{2,0},{3,1},{4,6},{5,7},{6,4},{7,5},{8,10},{9,11},{10,... | collective-permute-start | bytes 344072 | tf_op jit(solution)/shard_map/ppermute | solution.py:20
  14.7 3.5 %collective-permute-done.5 = bf16[224,256]{1,0:T(8,128)(2,1)S(1)} collective-permute-done((bf16[224,256]{1,0:T(8,128)(2,1)S(1)}, bf16[224,256]{1,0:T(8,128)(2,1)S(1)}, u32[]{:S(2)}, u32[]{:S(2)}) %collective-permute-start.5) | collective-permute-done | bytes 114720 | tf_op jit(solution)/shard_map/ppermute | solution.py:20
  19.5 1.5 %collective-permute-start.7 = (bf16[4,224,256]{2,1,0:T(8,128)(2,1)S(1)}, bf16[4,224,256]{2,1,0:T(8,128)(2,1)S(1)}, u32[]{:S(2)}, u32[]{:S(2)}) collective-permute-start(bf16[4,224,256]{2,1,0:T(8,128)(2,1)S(1)} %pad_maximum_fusion.refs_4_), channel_id=1, source_target_pairs={{0,12},{4,0},{8,4},{12,8},{1,13},{5,1},{9,5},{13,9},{2,14},{6,2},{... | collective-permute-start | bytes 1376264 | tf_op jit(solution)/shard_map/ppermute | solution.py:20
  21.0 1.6 %collective-permute-start.10 = (bf16[4,224,256]{2,1,0:T(8,128)(2,1)S(1)}, bf16[4,224,256]{2,1,0:T(8,128)(2,1)S(1)}, u32[]{:S(2)}, u32[]{:S(2)}) collective-permute-start(bf16[4,224,256]{2,1,0:T(8,128)(2,1)S(1)} %pad_maximum_fusion.refs_4_), channel_id=1, source_target_pairs={{0,16},{16,0},{1,17},{17,1},{2,18},{18,2},{3,19},{19,3},{4,20},{20... | collective-permute-start | bytes 1376264 | tf_op jit(solution)/shard_map/ppermute | solution.py:20
  22.6 8.2 %collective-permute-done.6.refs_5_ = bf16[4,224,256]{2,1,0:T(8,128)(2,1)S(1)} collective-permute-done((bf16[4,224,256]{2,1,0:T(8,128)(2,1)S(1)}, bf16[4,224,256]{2,1,0:T(8,128)(2,1)S(1)}, u32[]{:S(2)}, u32[]{:S(2)}) %collective-permute-start.6) | collective-permute-done | bytes 458784 | tf_op jit(solution)/shard_map/ppermute | solution.py:20
  32.2 2.7 %collective-permute-start.9 = (bf16[2,224,256]{2,1,0:T(8,128)(2,1)}, bf16[2,224,256]{2,1,0:T(8,128)(2,1)S(1)}, u32[]{:S(2)}, u32[]{:S(2)}) collective-permute-start(bf16[2,224,256]{2,1,0:T(8,128)(2,1)} %slice.9), channel_id=1, source_target_pairs={{0,12},{4,0},{8,4},{12,8},{1,13},{5,1},{9,5},{13,9},{2,14},{6,2},{... | collective-permute-start | bytes 688136 | tf_op jit(solution)/shard_map/ppermute | solution.py:20
  34.9 2.2 %dynamic-slice_bitcast_fusion = (bf16[224,640]{1,0:T(8,128)(2,1)}, bf16[224,640]{1,0:T(8,128)(2,1)S(1)}, bf16[224,640]{1,0:T(8,128)(2,1)S(1)}, bf16[224,640]{1,0:T(8,128)(2,1)}) fusion(bf16[1,224,2560]{2,1,0:T(8,128)(2,1)} %param.7, s32[]{:T(128)S(6)} %select_n.31, s32[]{:T(128)S(6)} %select_n.29, s32[]{:T(128)S(6)} %select_n.28, s32[]{:T(128)S(6)} %select_n.30), kind=kLoop, calls=%fused_computation.2 | loop fusion | bytes 2293776 | tf_op jit(solution)/shard_map/dynamic_slice | solution.py:296
  37.2 2.7 %collective-permute-start.12 = (bf16[4,224,256]{2,1,0:T(8,128)(2,1)S(1)}, bf16[4,224,256]{2,1,0:T(8,128)(2,1)S(1)}, u32[]{:S(2)}, u32[]{:S(2)}) collective-permute-start(bf16[4,224,256]{2,1,0:T(8,128)(2,1)S(1)} %collective-permute-done.10.refs_9_), channel_id=1, source_target_pairs={{0,12},{4,0},{8,4},{12,8},{1,13},{5,1},{9,5},{13,9},{2,14},{6,2},{... | collective-permute-start | bytes 1376264 | tf_op jit(solution)/shard_map/ppermute | solution.py:20
  40.7 1.5 %collective-permute-start.13 = (bf16[4,224,256]{2,1,0:T(8,128)(2,1)}, bf16[4,224,256]{2,1,0:T(8,128)(2,1)}, u32[]{:S(2)}, u32[]{:S(2)}) collective-permute-start(bf16[4,224,256]{2,1,0:T(8,128)(2,1)} %pad_maximum_fusion.1), channel_id=1, source_target_pairs={{0,16},{16,0},{1,17},{17,1},{2,18},{18,2},{3,19},{19,3},{4,20},{20... | collective-permute-start | bytes 1376264 | tf_op jit(solution)/shard_map/ppermute | solution.py:20
  42.2 2.6 %collective-permute-start.1 = (bf16[224,640]{1,0:T(8,128)(2,1)}, bf16[224,640]{1,0:T(8,128)(2,1)}, u32[]{:S(2)}, u32[]{:S(2)}) collective-permute-start(bf16[224,640]{1,0:T(8,128)(2,1)} %get-tuple-element.22), channel_id=1, source_target_pairs={{0,3},{1,0},{2,1},{3,2},{4,7},{5,4},{6,5},{7,6},{8,11},{9,8},{10,9... | collective-permute-start | bytes 860168 | tf_op jit(solution)/shard_map/ppermute | solution.py:20
  47.5 7.8 %collective-permute-done.1.refs_2_ = bf16[224,640]{1,0:T(8,128)(2,1)} collective-permute-done((bf16[224,640]{1,0:T(8,128)(2,1)}, bf16[224,640]{1,0:T(8,128)(2,1)}, u32[]{:S(2)}, u32[]{:S(2)}) %collective-permute-start.1) | collective-permute-done | bytes 286752 | tf_op jit(solution)/shard_map/ppermute | solution.py:20
  55.3 4.1 %collective-permute-done.2.refs_3_ = bf16[224,640]{1,0:T(8,128)(2,1)} collective-permute-done((bf16[224,640]{1,0:T(8,128)(2,1)}, bf16[224,640]{1,0:T(8,128)(2,1)}, u32[]{:S(2)}, u32[]{:S(2)}) %collective-permute-start.2) | collective-permute-done | bytes 286752 | tf_op jit(solution)/shard_map/ppermute | solution.py:20
  60.3 14.0 %attend.1 = (bf16[224,640]{1,0:T(8,128)(2,1)S(1)}, bf16[224,640]{1,0:T(8,128)(2,1)S(1)}, bf16[224,640]{1,0:T(8,128)(2,1)S(1)}, bf16[224,640]{1,0:T(8,128)(2,1)S(1)}) custom-call(s32[135]{0:T(256)S(1)} %concatenate.18.table, bf16[224,640]{1,0:T(8,128)(2,1)S(1)} %get-tuple-element.21.refs_0_, bf16[224,640]{1,0:T(8,128)(2,1)S(1)} %copy-done.2, ...), custom_call_target="tpu_custom_call" | custom-call | flops 8000000000 | bytes 6000000 | tf_op jit(solution)/shard_map/attend/pallas_call | solution.py:181
  74.4 4.7 %collective-permute-start.14 = (bf16[224,640]{1,0:T(8,128)(2,1)S(1)}, bf16[224,640]{1,0:T(8,128)(2,1)S(1)}, u32[]{:S(2)}, u32[]{:S(2)}) collective-permute-start(bf16[224,640]{1,0:T(8,128)(2,1)S(1)} %get-tuple-element.12), channel_id=1, source_target_pairs={{0,1},{1,2},{2,3},{3,0},{4,5},{5,6},{6,7},{7,4},{8,9},{9,10},{10,1... | collective-permute-start | bytes 860168 | tf_op jit(solution)/shard_map/ppermute | solution.py:20
  81.0 12.9 %collective-permute-start.17 = (bf16[224,640]{1,0:T(8,128)(2,1)S(1)}, bf16[224,640]{1,0:T(8,128)(2,1)S(1)}, u32[]{:S(2)}, u32[]{:S(2)}) collective-permute-start(bf16[224,640]{1,0:T(8,128)(2,1)S(1)} %get-tuple-element.11.refs_0_), channel_id=1, source_target_pairs={{0,32},{32,0},{1,33},{33,1},{2,34},{34,2},{3,35},{35,3},{4,36},{36... | collective-permute-start | bytes 860168 | tf_op jit(solution)/shard_map/ppermute | solution.py:20
  94.6 10.9 %collective-permute-start.18 = (bf16[224,640]{1,0:T(8,128)(2,1)S(1)}, bf16[224,640]{1,0:T(8,128)(2,1)S(1)}, u32[]{:S(2)}, u32[]{:S(2)}) collective-permute-start(bf16[224,640]{1,0:T(8,128)(2,1)S(1)} %collective-permute-done.14.refs_1_), channel_id=1, source_target_pairs={{0,32},{32,0},{1,33},{33,1},{2,34},{34,2},{3,35},{35,3},{4,36},{36... | collective-permute-start | bytes 860168 | tf_op jit(solution)/shard_map/ppermute | solution.py:20
  105.8 10.0 %collective-permute-start.20 = (bf16[224,640]{1,0:T(8,128)(2,1)S(1)}, bf16[224,640]{1,0:T(8,128)(2,1)S(1)}, u32[]{:S(2)}, u32[]{:S(2)}) collective-permute-start(bf16[224,640]{1,0:T(8,128)(2,1)S(1)} %collective-permute-done.16.refs_3_), channel_id=1, source_target_pairs={{0,32},{32,0},{1,33},{33,1},{2,34},{34,2},{3,35},{35,3},{4,36},{36... | collective-permute-start | bytes 860168 | tf_op jit(solution)/shard_map/ppermute | solution.py:20
  116.9 8.1 %all-gather.2.cloned.1.call-done.refs_8_ = bf16[5120,1280]{1,0:T(8,128)(2,1)} async-done(((bf16[80,1280]{1,0:T(8,128)(2,1)}), bf16[5120,1280]{1,0:T(8,128)(2,1)}) %all-gather.2.cloned.1.call-update) | async-done | bytes 13107216 | tf_op jit(solution)/shard_map/all_gather | solution.py:298
  125.0 4.7 %copy-done = bf16[5120,1280]{1,0:T(8,128)(2,1)S(1)} copy-done((bf16[5120,1280]{1,0:T(8,128)(2,1)S(1)}, bf16[5120,1280]{1,0:T(8,128)(2,1)}, u32[]{:S(2)}) %copy-start) | copy-done | bytes 13107224
  130.7 7.8 %project.1 = (bf16[224,5120]{1,0:T(8,128)(2,1)}, bf16[2,224,1280]{2,1,0:T(8,128)(2,1)S(1)}) custom-call(s32[135]{0:T(256)S(1)} %concatenate.18.table, bf16[224,640]{1,0:T(8,128)(2,1)S(1)} %copy-done.4, bf16[224,640]{1,0:T(8,128)(2,1)S(1)} %collective-permute-done.14.refs_1_, bf16[224,640]{1,0:T(8,128)(2,1)S(1)} %collective-permute-done.15.refs_2_, ...), custom_call_target="tpu_custom_call" | custom-call | flops 6000000000 | bytes 18000000 | tf_op jit(solution)/shard_map/project/pallas_call | solution.py:227
  139.2 2.4 %collective-permute-done.21.theirs = bf16[2,224,1280]{2,1,0:T(8,128)(2,1)S(1)} collective-permute-done((bf16[2,224,1280]{2,1,0:T(8,128)(2,1)S(1)}, bf16[2,224,1280]{2,1,0:T(8,128)(2,1)S(1)}, u32[]{:S(2)}, u32[]{:S(2)}) %collective-permute-start.21) | collective-permute-done | bytes 1146912 | tf_op jit(solution)/shard_map/ppermute | solution.py:20
  141.6 1.6 %merge.1 = bf16[224,5120]{1,0:T(8,128)(2,1)} custom-call(s32[135]{0:T(256)S(1)} %concatenate.18.table, bf16[2,224,1280]{2,1,0:T(8,128)(2,1)S(1)} %collective-permute-done.21.theirs, bf16[224,5120]{1,0:T(8,128)(2,1)} %get-tuple-element.16.whole), custom_call_target="tpu_custom_call", output_to_operand_aliasing={{}: (2, {})} | custom-call | bytes 3000000 | tf_op jit(solution)/shard_map/merge/pallas_call | solution.py:267
  (54 shorter events, 15.7 us)
Async XLA Ops:
  6.5 118.5 %all-gather.2.cloned.1.call-start = ((), (), s32[]{:S(2)}) async-start(), calls=%async_computation | async-start | bytes 13312000 | tf_op jit(solution)/shard_map/all_gather | solution.py:298
  8.4 6.4 %collective-permute-start.3 = (bf16[224,256]{1,0:T(8,128)(2,1)S(1)}, bf16[224,256]{1,0:T(8,128)(2,1)S(1)}, u32[]{:S(2)}, u32[]{:S(2)}) collective-permute-start(bf16[224,256]{1,0:T(8,128)(2,1)S(1)} %pad_maximum_fusion.2), channel_id=1, source_target_pairs={{0,1},{1,2},{2,3},{3,0},{4,5},{5,6},{6,7},{7,4},{8,9},{9,10},{10,1... | collective-permute-start | bytes 344072 | tf_op jit(solution)/shard_map/ppermute | solution.py:20
  10.6 4.1 %collective-permute-start.4 = (bf16[224,256]{1,0:T(8,128)(2,1)S(1)}, bf16[224,256]{1,0:T(8,128)(2,1)S(1)}, u32[]{:S(2)}, u32[]{:S(2)}) collective-permute-start(bf16[224,256]{1,0:T(8,128)(2,1)S(1)} %pad_maximum_fusion.3), channel_id=1, source_target_pairs={{0,3},{1,0},{2,1},{3,2},{4,7},{5,4},{6,5},{7,6},{8,11},{9,8},{10,9... | collective-permute-start | bytes 344072 | tf_op jit(solution)/shard_map/ppermute | solution.py:20
  12.1 6.1 %collective-permute-start.5 = (bf16[224,256]{1,0:T(8,128)(2,1)S(1)}, bf16[224,256]{1,0:T(8,128)(2,1)S(1)}, u32[]{:S(2)}, u32[]{:S(2)}) collective-permute-start(bf16[224,256]{1,0:T(8,128)(2,1)S(1)} %pad_maximum_fusion.4), channel_id=1, source_target_pairs={{0,2},{1,3},{2,0},{3,1},{4,6},{5,7},{6,4},{7,5},{8,10},{9,11},{10,... | collective-permute-start | bytes 344072 | tf_op jit(solution)/shard_map/ppermute | solution.py:20
  18.3 12.5 %collective-permute-start.6 = (bf16[4,224,256]{2,1,0:T(8,128)(2,1)S(1)}, bf16[4,224,256]{2,1,0:T(8,128)(2,1)S(1)}, u32[]{:S(2)}, u32[]{:S(2)}) collective-permute-start(bf16[4,224,256]{2,1,0:T(8,128)(2,1)S(1)} %pad_maximum_fusion.refs_4_), channel_id=1, source_target_pairs={{0,4},{4,8},{8,12},{12,0},{1,5},{5,9},{9,13},{13,1},{2,6},{6,10},{... | collective-permute-start | bytes 1376264 | tf_op jit(solution)/shard_map/ppermute | solution.py:20
  19.5 12.0 %collective-permute-start.7 = (bf16[4,224,256]{2,1,0:T(8,128)(2,1)S(1)}, bf16[4,224,256]{2,1,0:T(8,128)(2,1)S(1)}, u32[]{:S(2)}, u32[]{:S(2)}) collective-permute-start(bf16[4,224,256]{2,1,0:T(8,128)(2,1)S(1)} %pad_maximum_fusion.refs_4_), channel_id=1, source_target_pairs={{0,12},{4,0},{8,4},{12,8},{1,13},{5,1},{9,5},{13,9},{2,14},{6,2},{... | collective-permute-start | bytes 1376264 | tf_op jit(solution)/shard_map/ppermute | solution.py:20
  21.0 16.1 %collective-permute-start.10 = (bf16[4,224,256]{2,1,0:T(8,128)(2,1)S(1)}, bf16[4,224,256]{2,1,0:T(8,128)(2,1)S(1)}, u32[]{:S(2)}, u32[]{:S(2)}) collective-permute-start(bf16[4,224,256]{2,1,0:T(8,128)(2,1)S(1)} %pad_maximum_fusion.refs_4_), channel_id=1, source_target_pairs={{0,16},{16,0},{1,17},{17,1},{2,18},{18,2},{3,19},{19,3},{4,20},{20... | collective-permute-start | bytes 1376264 | tf_op jit(solution)/shard_map/ppermute | solution.py:20
  31.5 8.3 %collective-permute-start.8 = (bf16[2,224,256]{2,1,0:T(8,128)(2,1)}, bf16[2,224,256]{2,1,0:T(8,128)(2,1)S(1)}, u32[]{:S(2)}, u32[]{:S(2)}) collective-permute-start(bf16[2,224,256]{2,1,0:T(8,128)(2,1)} %slice.8), channel_id=1, source_target_pairs={{0,4},{4,8},{8,12},{12,0},{1,5},{5,9},{9,13},{13,1},{2,6},{6,10},{... | collective-permute-start | bytes 688136 | tf_op jit(solution)/shard_map/ppermute | solution.py:20
  32.2 7.6 %collective-permute-start.9 = (bf16[2,224,256]{2,1,0:T(8,128)(2,1)}, bf16[2,224,256]{2,1,0:T(8,128)(2,1)S(1)}, u32[]{:S(2)}, u32[]{:S(2)}) collective-permute-start(bf16[2,224,256]{2,1,0:T(8,128)(2,1)} %slice.9), channel_id=1, source_target_pairs={{0,12},{4,0},{8,4},{12,8},{1,13},{5,1},{9,5},{13,9},{2,14},{6,2},{... | collective-permute-start | bytes 688136 | tf_op jit(solution)/shard_map/ppermute | solution.py:20
  34.9 11.3 %copy-start.7 = (s32[1,64]{1,0:T(1,128)S(1)}, s32[1,64]{1,0:T(1,128)}, u32[]{:S(2)}) copy-start(s32[1,64]{1,0:T(1,128)} %param.11) | copy-start | bytes 772
  37.1 7.7 %collective-permute-start = (bf16[224,640]{1,0:T(8,128)(2,1)S(1)}, bf16[224,640]{1,0:T(8,128)(2,1)S(1)}, u32[]{:S(2)}, u32[]{:S(2)}) collective-permute-start(bf16[224,640]{1,0:T(8,128)(2,1)S(1)} %get-tuple-element.20), channel_id=1, source_target_pairs={{0,1},{1,2},{2,3},{3,0},{4,5},{5,6},{6,7},{7,4},{8,9},{9,10},{10,1... | collective-permute-start | bytes 860168 | tf_op jit(solution)/shard_map/ppermute | solution.py:20
  37.1 22.3 %collective-permute-start.11 = (bf16[4,224,256]{2,1,0:T(8,128)(2,1)S(1)}, bf16[4,224,256]{2,1,0:T(8,128)(2,1)S(1)}, u32[]{:S(2)}, u32[]{:S(2)}) collective-permute-start(bf16[4,224,256]{2,1,0:T(8,128)(2,1)S(1)} %collective-permute-done.10.refs_9_), channel_id=1, source_target_pairs={{0,4},{4,8},{8,12},{12,0},{1,5},{5,9},{9,13},{13,1},{2,6},{6,10},{... | collective-permute-start | bytes 1376264 | tf_op jit(solution)/shard_map/ppermute | solution.py:20
  37.2 22.2 %collective-permute-start.12 = (bf16[4,224,256]{2,1,0:T(8,128)(2,1)S(1)}, bf16[4,224,256]{2,1,0:T(8,128)(2,1)S(1)}, u32[]{:S(2)}, u32[]{:S(2)}) collective-permute-start(bf16[4,224,256]{2,1,0:T(8,128)(2,1)S(1)} %collective-permute-done.10.refs_9_), channel_id=1, source_target_pairs={{0,12},{4,0},{8,4},{12,8},{1,13},{5,1},{9,5},{13,9},{2,14},{6,2},{... | collective-permute-start | bytes 1376264 | tf_op jit(solution)/shard_map/ppermute | solution.py:20
  40.7 18.7 %collective-permute-start.13 = (bf16[4,224,256]{2,1,0:T(8,128)(2,1)}, bf16[4,224,256]{2,1,0:T(8,128)(2,1)}, u32[]{:S(2)}, u32[]{:S(2)}) collective-permute-start(bf16[4,224,256]{2,1,0:T(8,128)(2,1)} %pad_maximum_fusion.1), channel_id=1, source_target_pairs={{0,16},{16,0},{1,17},{17,1},{2,18},{18,2},{3,19},{19,3},{4,20},{20... | collective-permute-start | bytes 1376264 | tf_op jit(solution)/shard_map/ppermute | solution.py:20
  42.2 13.1 %collective-permute-start.1 = (bf16[224,640]{1,0:T(8,128)(2,1)}, bf16[224,640]{1,0:T(8,128)(2,1)}, u32[]{:S(2)}, u32[]{:S(2)}) collective-permute-start(bf16[224,640]{1,0:T(8,128)(2,1)} %get-tuple-element.22), channel_id=1, source_target_pairs={{0,3},{1,0},{2,1},{3,2},{4,7},{5,4},{6,5},{7,6},{8,11},{9,8},{10,9... | collective-permute-start | bytes 860168 | tf_op jit(solution)/shard_map/ppermute | solution.py:20
  45.5 13.9 %collective-permute-start.2 = (bf16[224,640]{1,0:T(8,128)(2,1)}, bf16[224,640]{1,0:T(8,128)(2,1)}, u32[]{:S(2)}, u32[]{:S(2)}) collective-permute-start(bf16[224,640]{1,0:T(8,128)(2,1)} %get-tuple-element.19), channel_id=1, source_target_pairs={{0,2},{1,3},{2,0},{3,1},{4,6},{5,7},{6,4},{7,5},{8,10},{9,11},{10,... | collective-permute-start | bytes 860168 | tf_op jit(solution)/shard_map/ppermute | solution.py:20
  74.4 20.3 %collective-permute-start.14 = (bf16[224,640]{1,0:T(8,128)(2,1)S(1)}, bf16[224,640]{1,0:T(8,128)(2,1)S(1)}, u32[]{:S(2)}, u32[]{:S(2)}) collective-permute-start(bf16[224,640]{1,0:T(8,128)(2,1)S(1)} %get-tuple-element.12), channel_id=1, source_target_pairs={{0,1},{1,2},{2,3},{3,0},{4,5},{5,6},{6,7},{7,4},{8,9},{9,10},{10,1... | collective-permute-start | bytes 860168 | tf_op jit(solution)/shard_map/ppermute | solution.py:20
  79.1 26.5 %collective-permute-start.15 = (bf16[224,640]{1,0:T(8,128)(2,1)S(1)}, bf16[224,640]{1,0:T(8,128)(2,1)S(1)}, u32[]{:S(2)}, u32[]{:S(2)}) collective-permute-start(bf16[224,640]{1,0:T(8,128)(2,1)S(1)} %get-tuple-element.13), channel_id=1, source_target_pairs={{0,3},{1,0},{2,1},{3,2},{4,7},{5,4},{6,5},{7,6},{8,11},{9,8},{10,9... | collective-permute-start | bytes 860168 | tf_op jit(solution)/shard_map/ppermute | solution.py:20
  79.9 25.8 %collective-permute-start.16 = (bf16[224,640]{1,0:T(8,128)(2,1)S(1)}, bf16[224,640]{1,0:T(8,128)(2,1)S(1)}, u32[]{:S(2)}, u32[]{:S(2)}) collective-permute-start(bf16[224,640]{1,0:T(8,128)(2,1)S(1)} %get-tuple-element.14), channel_id=1, source_target_pairs={{0,2},{1,3},{2,0},{3,1},{4,6},{5,7},{6,4},{7,5},{8,10},{9,11},{10,... | collective-permute-start | bytes 860168 | tf_op jit(solution)/shard_map/ppermute | solution.py:20
  81.0 34.7 %collective-permute-start.17 = (bf16[224,640]{1,0:T(8,128)(2,1)S(1)}, bf16[224,640]{1,0:T(8,128)(2,1)S(1)}, u32[]{:S(2)}, u32[]{:S(2)}) collective-permute-start(bf16[224,640]{1,0:T(8,128)(2,1)S(1)} %get-tuple-element.11.refs_0_), channel_id=1, source_target_pairs={{0,32},{32,0},{1,33},{33,1},{2,34},{34,2},{3,35},{35,3},{4,36},{36... | collective-permute-start | bytes 860168 | tf_op jit(solution)/shard_map/ppermute | solution.py:20
  94.6 21.1 %collective-permute-start.18 = (bf16[224,640]{1,0:T(8,128)(2,1)S(1)}, bf16[224,640]{1,0:T(8,128)(2,1)S(1)}, u32[]{:S(2)}, u32[]{:S(2)}) collective-permute-start(bf16[224,640]{1,0:T(8,128)(2,1)S(1)} %collective-permute-done.14.refs_1_), channel_id=1, source_target_pairs={{0,32},{32,0},{1,33},{33,1},{2,34},{34,2},{3,35},{35,3},{4,36},{36... | collective-permute-start | bytes 860168 | tf_op jit(solution)/shard_map/ppermute | solution.py:20
  105.6 10.2 %collective-permute-start.19 = (bf16[224,640]{1,0:T(8,128)(2,1)S(1)}, bf16[224,640]{1,0:T(8,128)(2,1)S(1)}, u32[]{:S(2)}, u32[]{:S(2)}) collective-permute-start(bf16[224,640]{1,0:T(8,128)(2,1)S(1)} %collective-permute-done.15.refs_2_), channel_id=1, source_target_pairs={{0,32},{32,0},{1,33},{33,1},{2,34},{34,2},{3,35},{35,3},{4,36},{36... | collective-permute-start | bytes 860168 | tf_op jit(solution)/shard_map/ppermute | solution.py:20
  105.8 11.2 %collective-permute-start.20 = (bf16[224,640]{1,0:T(8,128)(2,1)S(1)}, bf16[224,640]{1,0:T(8,128)(2,1)S(1)}, u32[]{:S(2)}, u32[]{:S(2)}) collective-permute-start(bf16[224,640]{1,0:T(8,128)(2,1)S(1)} %collective-permute-done.16.refs_3_), channel_id=1, source_target_pairs={{0,32},{32,0},{1,33},{33,1},{2,34},{34,2},{3,35},{35,3},{4,36},{36... | collective-permute-start | bytes 860168 | tf_op jit(solution)/shard_map/ppermute | solution.py:20
  138.5 3.1 %collective-permute-start.21 = (bf16[2,224,1280]{2,1,0:T(8,128)(2,1)S(1)}, bf16[2,224,1280]{2,1,0:T(8,128)(2,1)S(1)}, u32[]{:S(2)}, u32[]{:S(2)}) collective-permute-start(bf16[2,224,1280]{2,1,0:T(8,128)(2,1)S(1)} %get-tuple-element.15), channel_id=1, source_target_pairs={{0,32},{32,0},{1,33},{33,1},{2,34},{34,2},{3,35},{35,3},{4,36},{36... | collective-permute-start | bytes 3440648 | tf_op jit(solution)/shard_map/ppermute | solution.py:20
  (7 other events, 30.0 us)
Sparse Core Ops, SparseCore 0:
  10.2 114.7 all-gather.1

commit v3 on v2

--- a/solution.py
+++ b/solution.py
@@ -240,7 +240,7 @@
             ],
             scratch_shapes=[pltpu.VMEM((2 * tok, rows), jnp.bfloat16)],
         ),
-        compiler_params=pltpu.CompilerParams(vmem_limit_bytes=32 * 2**20),
+        compiler_params=pltpu.CompilerParams(vmem_limit_bytes=48 * 2**20),
         cost_estimate=pl.CostEstimate(
             flops=6 * 10**9, bytes_accessed=18 * 10**6, transcendentals=0
         ),

time: 150 us -> 149 us (level)
  starting transfers between devices: 60.6 us -> 39.9 us
  waiting for transfers between devices: 36.9 us -> 55.4 us
  Pallas kernels: 23.4 us -> 28.5 us
  local copies, waits for them, and re-layouts: 14 us -> 9.33 us
    ppermute x22, starting transfers between devices: 60.6 us -> 39.9 us  [shifted(): lax.ppermute(array, axis, [(i, (i + step) % size) for i in range(size)])]
    ppermute x22, waiting for transfers between devices: 28.1 us -> 42.7 us  [shifted(): lax.ppermute(array, axis, [(i, (i + step) % size) for i in range(size)])]
    unnamed x16 -> x14, local copies, waits for them, and re-layouts: 8.06 us -> 3.36 us
    all_gather x1, waiting for transfers between devices: 8.07 us -> 12 us  [per_device(): lax.all_gather(out_weight, ('zh', 'zl', 'x', 'y'), axis=0, tiled=True)]
    pallas_call x1, Pallas kernels: 7.84 us -> 10.7 us  [project(): pl.pallas_call(functools.partial(project_kernel, base), out_shape=[jax.Sh...]
    pallas_call x1, Pallas kernels: 14 us -> 16.2 us  [attention(): pl.pallas_call(functools.partial(attention_kernel, groups, sec, nsec, shi...]
  transfers between devices with their start and end apart: 23 -> 23, of which waited for: 8 -> 10; matrix products, arithmetic and copies ran while one was open for 5% -> 5% of each run, Pallas kernels for 9% -> 11%
where the time goes in v3:
time: 149 us; the launch traced here: 148 us
  waiting for transfers between devices  55.4 us (37%)
  starting transfers between devices  39.9 us (27%)
  Pallas kernels  28.5 us (19%)
  between operations  13.5 us (9%)
  local copies, waits for them, and re-layouts  9.33 us (6%)
  other arithmetic  1.65 us (1%)
    ppermute x22, waiting for transfers between devices, shifted(): lax.ppermute(array, axis, [(i, (i + step) % size) for i in range(size)])  42.7 us
    ppermute x22, starting transfers between devices, shifted(): lax.ppermute(array, axis, [(i, (i + step) % size) for i in range(size)])  39.9 us
    pallas_call x1, Pallas kernels, attention(): pl.pallas_call(functools.partial(attention_kernel, groups, sec, nsec, shi...  16.2 us
    all_gather x1, waiting for transfers between devices, per_device(): lax.all_gather(out_weight, ('zh', 'zl', 'x', 'y'), axis=0, tiled=True)  12 us
    pallas_call x1, Pallas kernels, project(): pl.pallas_call(functools.partial(project_kernel, base), out_shape=[jax.Sh...  10.7 us
    unnamed x14, local copies, waits for them, and re-layouts  3.36 us
    dynamic_slice x2, local copies, waits for them, and re-layouts, head_slice(): return lax.dynamic_slice_in_dim(array[0], wrap(y + shift) * wide, wide, 1)  3.24 us
  transfers between devices with their start and end apart: 23, of which 10 were waited for; matrix products, arithmetic and copies ran while one was open for 5% of the time, Pallas kernels for 11%

profile of v3, /device:TPU:1, one launch (start us, length us, event | category | flops | bytes accessed | tf_op | source)
XLA Modules:
  0.0 148.2 jit_solution(3666342159554186741)
XLA Ops:
  8.4 2.2 %collective-permute-start.3 = (bf16[224,256]{1,0:T(8,128)(2,1)S(1)}, bf16[224,256]{1,0:T(8,128)(2,1)S(1)}, u32[]{:S(2)}, u32[]{:S(2)}) collective-permute-start(bf16[224,256]{1,0:T(8,128)(2,1)S(1)} %pad_maximum_fusion.2), channel_id=1, source_target_pairs={{0,1},{1,2},{2,3},{3,0},{4,5},{5,6},{6,7},{7,4},{8,9},{9,10},{10,1... | collective-permute-start | bytes 344072 | tf_op jit(solution)/shard_map/ppermute | solution.py:20
  12.1 1.7 %collective-permute-start.5 = (bf16[224,256]{1,0:T(8,128)(2,1)S(1)}, bf16[224,256]{1,0:T(8,128)(2,1)S(1)}, u32[]{:S(2)}, u32[]{:S(2)}) collective-permute-start(bf16[224,256]{1,0:T(8,128)(2,1)S(1)} %pad_maximum_fusion.4), channel_id=1, source_target_pairs={{0,2},{1,3},{2,0},{3,1},{4,6},{5,7},{6,4},{7,5},{8,10},{9,11},{10,... | collective-permute-start | bytes 344072 | tf_op jit(solution)/shard_map/ppermute | solution.py:20
  14.7 3.5 %collective-permute-done.5 = bf16[224,256]{1,0:T(8,128)(2,1)S(1)} collective-permute-done((bf16[224,256]{1,0:T(8,128)(2,1)S(1)}, bf16[224,256]{1,0:T(8,128)(2,1)S(1)}, u32[]{:S(2)}, u32[]{:S(2)}) %collective-permute-start.5) | collective-permute-done | bytes 114720 | tf_op jit(solution)/shard_map/ppermute | solution.py:20
  19.5 1.5 %collective-permute-start.7 = (bf16[4,224,256]{2,1,0:T(8,128)(2,1)S(1)}, bf16[4,224,256]{2,1,0:T(8,128)(2,1)S(1)}, u32[]{:S(2)}, u32[]{:S(2)}) collective-permute-start(bf16[4,224,256]{2,1,0:T(8,128)(2,1)S(1)} %pad_maximum_fusion.refs_4_), channel_id=1, source_target_pairs={{0,12},{4,0},{8,4},{12,8},{1,13},{5,1},{9,5},{13,9},{2,14},{6,2},{... | collective-permute-start | bytes 1376264 | tf_op jit(solution)/shard_map/ppermute | solution.py:20
  21.0 1.6 %collective-permute-start.10 = (bf16[4,224,256]{2,1,0:T(8,128)(2,1)S(1)}, bf16[4,224,256]{2,1,0:T(8,128)(2,1)S(1)}, u32[]{:S(2)}, u32[]{:S(2)}) collective-permute-start(bf16[4,224,256]{2,1,0:T(8,128)(2,1)S(1)} %pad_maximum_fusion.refs_4_), channel_id=1, source_target_pairs={{0,16},{16,0},{1,17},{17,1},{2,18},{18,2},{3,19},{19,3},{4,20},{20... | collective-permute-start | bytes 1376264 | tf_op jit(solution)/shard_map/ppermute | solution.py:20
  22.6 8.2 %collective-permute-done.6.refs_5_ = bf16[4,224,256]{2,1,0:T(8,128)(2,1)S(1)} collective-permute-done((bf16[4,224,256]{2,1,0:T(8,128)(2,1)S(1)}, bf16[4,224,256]{2,1,0:T(8,128)(2,1)S(1)}, u32[]{:S(2)}, u32[]{:S(2)}) %collective-permute-start.6) | collective-permute-done | bytes 458784 | tf_op jit(solution)/shard_map/ppermute | solution.py:20
  32.2 2.7 %collective-permute-start.9 = (bf16[2,224,256]{2,1,0:T(8,128)(2,1)}, bf16[2,224,256]{2,1,0:T(8,128)(2,1)S(1)}, u32[]{:S(2)}, u32[]{:S(2)}) collective-permute-start(bf16[2,224,256]{2,1,0:T(8,128)(2,1)} %slice.9), channel_id=1, source_target_pairs={{0,12},{4,0},{8,4},{12,8},{1,13},{5,1},{9,5},{13,9},{2,14},{6,2},{... | collective-permute-start | bytes 688136 | tf_op jit(solution)/shard_map/ppermute | solution.py:20
  34.9 2.2 %dynamic-slice_bitcast_fusion = (bf16[224,640]{1,0:T(8,128)(2,1)}, bf16[224,640]{1,0:T(8,128)(2,1)S(1)}, bf16[224,640]{1,0:T(8,128)(2,1)S(1)}, bf16[224,640]{1,0:T(8,128)(2,1)}) fusion(bf16[1,224,2560]{2,1,0:T(8,128)(2,1)} %param.7, s32[]{:T(128)S(6)} %select_n.31, s32[]{:T(128)S(6)} %select_n.29, s32[]{:T(128)S(6)} %select_n.28, s32[]{:T(128)S(6)} %select_n.30), kind=kLoop, calls=%fused_computation.2 | loop fusion | bytes 2293776 | tf_op jit(solution)/shard_map/dynamic_slice | solution.py:296
  37.2 2.7 %collective-permute-start.12 = (bf16[4,224,256]{2,1,0:T(8,128)(2,1)S(1)}, bf16[4,224,256]{2,1,0:T(8,128)(2,1)S(1)}, u32[]{:S(2)}, u32[]{:S(2)}) collective-permute-start(bf16[4,224,256]{2,1,0:T(8,128)(2,1)S(1)} %collective-permute-done.10.refs_9_), channel_id=1, source_target_pairs={{0,12},{4,0},{8,4},{12,8},{1,13},{5,1},{9,5},{13,9},{2,14},{6,2},{... | collective-permute-start | bytes 1376264 | tf_op jit(solution)/shard_map/ppermute | solution.py:20
  40.7 1.5 %collective-permute-start.13 = (bf16[4,224,256]{2,1,0:T(8,128)(2,1)}, bf16[4,224,256]{2,1,0:T(8,128)(2,1)}, u32[]{:S(2)}, u32[]{:S(2)}) collective-permute-start(bf16[4,224,256]{2,1,0:T(8,128)(2,1)} %pad_maximum_fusion.1), channel_id=1, source_target_pairs={{0,16},{16,0},{1,17},{17,1},{2,18},{18,2},{3,19},{19,3},{4,20},{20... | collective-permute-start | bytes 1376264 | tf_op jit(solution)/shard_map/ppermute | solution.py:20
  42.2 2.6 %collective-permute-start.1 = (bf16[224,640]{1,0:T(8,128)(2,1)}, bf16[224,640]{1,0:T(8,128)(2,1)}, u32[]{:S(2)}, u32[]{:S(2)}) collective-permute-start(bf16[224,640]{1,0:T(8,128)(2,1)} %get-tuple-element.22), channel_id=1, source_target_pairs={{0,3},{1,0},{2,1},{3,2},{4,7},{5,4},{6,5},{7,6},{8,11},{9,8},{10,9... | collective-permute-start | bytes 860168 | tf_op jit(solution)/shard_map/ppermute | solution.py:20
  47.6 7.8 %collective-permute-done.1.refs_2_ = bf16[224,640]{1,0:T(8,128)(2,1)} collective-permute-done((bf16[224,640]{1,0:T(8,128)(2,1)}, bf16[224,640]{1,0:T(8,128)(2,1)}, u32[]{:S(2)}, u32[]{:S(2)}) %collective-permute-start.1) | collective-permute-done | bytes 286752 | tf_op jit(solution)/shard_map/ppermute | solution.py:20
  55.3 4.0 %collective-permute-done.2.refs_3_ = bf16[224,640]{1,0:T(8,128)(2,1)} collective-permute-done((bf16[224,640]{1,0:T(8,128)(2,1)}, bf16[224,640]{1,0:T(8,128)(2,1)}, u32[]{:S(2)}, u32[]{:S(2)}) %collective-permute-start.2) | collective-permute-done | bytes 286752 | tf_op jit(solution)/shard_map/ppermute | solution.py:20
  60.3 16.2 %attend.1 = (bf16[224,640]{1,0:T(8,128)(2,1)S(1)}, bf16[224,640]{1,0:T(8,128)(2,1)S(1)}, bf16[224,640]{1,0:T(8,128)(2,1)S(1)}, bf16[224,640]{1,0:T(8,128)(2,1)S(1)}) custom-call(s32[135]{0:T(256)S(1)} %concatenate.18.table, bf16[224,640]{1,0:T(8,128)(2,1)S(1)} %get-tuple-element.21.refs_0_, bf16[224,640]{1,0:T(8,128)(2,1)S(1)} %copy-done.1, ...), custom_call_target="tpu_custom_call" | custom-call | flops 8000000000 | bytes 6000000 | tf_op jit(solution)/shard_map/attend/pallas_call | solution.py:181
  76.6 4.7 %collective-permute-start.14 = (bf16[224,640]{1,0:T(8,128)(2,1)S(1)}, bf16[224,640]{1,0:T(8,128)(2,1)S(1)}, u32[]{:S(2)}, u32[]{:S(2)}) collective-permute-start(bf16[224,640]{1,0:T(8,128)(2,1)S(1)} %get-tuple-element.12), channel_id=1, source_target_pairs={{0,1},{1,2},{2,3},{3,0},{4,5},{5,6},{6,7},{7,4},{8,9},{9,10},{10,1... | collective-permute-start | bytes 860168 | tf_op jit(solution)/shard_map/ppermute | solution.py:20
  83.2 3.8 %collective-permute-start.17 = (bf16[224,640]{1,0:T(8,128)(2,1)S(1)}, bf16[224,640]{1,0:T(8,128)(2,1)S(1)}, u32[]{:S(2)}, u32[]{:S(2)}) collective-permute-start(bf16[224,640]{1,0:T(8,128)(2,1)S(1)} %get-tuple-element.11.refs_0_), channel_id=1, source_target_pairs={{0,32},{32,0},{1,33},{33,1},{2,34},{34,2},{3,35},{35,3},{4,36},{36... | collective-permute-start | bytes 860168 | tf_op jit(solution)/shard_map/ppermute | solution.py:20
  87.7 6.8 %collective-permute-done.14.refs_1_ = bf16[224,640]{1,0:T(8,128)(2,1)S(1)} collective-permute-done((bf16[224,640]{1,0:T(8,128)(2,1)S(1)}, bf16[224,640]{1,0:T(8,128)(2,1)S(1)}, u32[]{:S(2)}, u32[]{:S(2)}) %collective-permute-start.14) | collective-permute-done | bytes 286752 | tf_op jit(solution)/shard_map/ppermute | solution.py:20
  94.5 4.4 %collective-permute-start.18 = (bf16[224,640]{1,0:T(8,128)(2,1)S(1)}, bf16[224,640]{1,0:T(8,128)(2,1)S(1)}, u32[]{:S(2)}, u32[]{:S(2)}) collective-permute-start(bf16[224,640]{1,0:T(8,128)(2,1)S(1)} %collective-permute-done.14.refs_1_), channel_id=1, source_target_pairs={{0,32},{32,0},{1,33},{33,1},{2,34},{34,2},{3,35},{35,3},{4,36},{36... | collective-permute-start | bytes 860168 | tf_op jit(solution)/shard_map/ppermute | solution.py:20
  99.9 7.8 %collective-permute-done.16.refs_3_ = bf16[224,640]{1,0:T(8,128)(2,1)S(1)} collective-permute-done((bf16[224,640]{1,0:T(8,128)(2,1)S(1)}, bf16[224,640]{1,0:T(8,128)(2,1)S(1)}, u32[]{:S(2)}, u32[]{:S(2)}) %collective-permute-start.16) | collective-permute-done | bytes 286752 | tf_op jit(solution)/shard_map/ppermute | solution.py:20
  107.8 4.1 %collective-permute-start.20 = (bf16[224,640]{1,0:T(8,128)(2,1)S(1)}, bf16[224,640]{1,0:T(8,128)(2,1)S(1)}, u32[]{:S(2)}, u32[]{:S(2)}) collective-permute-start(bf16[224,640]{1,0:T(8,128)(2,1)S(1)} %collective-permute-done.16.refs_3_), channel_id=1, source_target_pairs={{0,32},{32,0},{1,33},{33,1},{2,34},{34,2},{3,35},{35,3},{4,36},{36... | collective-permute-start | bytes 860168 | tf_op jit(solution)/shard_map/ppermute | solution.py:20
  113.0 12.0 %all-gather.2.cloned.1.call-done.refs_8_ = bf16[5120,1280]{1,0:T(8,128)(2,1)} async-done(((bf16[80,1280]{1,0:T(8,128)(2,1)}), bf16[5120,1280]{1,0:T(8,128)(2,1)}) %all-gather.2.cloned.1.call-update) | async-done | bytes 13107216 | tf_op jit(solution)/shard_map/all_gather | solution.py:298
  126.0 10.7 %project.1 = (bf16[224,5120]{1,0:T(8,128)(2,1)}, bf16[2,224,1280]{2,1,0:T(8,128)(2,1)S(1)}) custom-call(s32[135]{0:T(256)S(1)} %concatenate.18.table, bf16[224,640]{1,0:T(8,128)(2,1)S(1)} %copy-done.3, bf16[224,640]{1,0:T(8,128)(2,1)S(1)} %collective-permute-done.14.refs_1_, bf16[224,640]{1,0:T(8,128)(2,1)S(1)} %collective-permute-done.15.refs_2_, ...), custom_call_target="tpu_custom_call" | custom-call | flops 6000000000 | bytes 18000000 | tf_op jit(solution)/shard_map/project/pallas_call | solution.py:227
  137.4 2.4 %collective-permute-done.21.theirs = bf16[2,224,1280]{2,1,0:T(8,128)(2,1)S(1)} collective-permute-done((bf16[2,224,1280]{2,1,0:T(8,128)(2,1)S(1)}, bf16[2,224,1280]{2,1,0:T(8,128)(2,1)S(1)}, u32[]{:S(2)}, u32[]{:S(2)}) %collective-permute-start.21) | collective-permute-done | bytes 1146912 | tf_op jit(solution)/shard_map/ppermute | solution.py:20
  139.8 1.6 %merge.1 = bf16[224,5120]{1,0:T(8,128)(2,1)} custom-call(s32[135]{0:T(256)S(1)} %concatenate.18.table, bf16[2,224,1280]{2,1,0:T(8,128)(2,1)S(1)} %collective-permute-done.21.theirs, bf16[224,5120]{1,0:T(8,128)(2,1)} %get-tuple-element.16.whole), custom_call_target="tpu_custom_call", output_to_operand_aliasing={{}: (2, {})} | custom-call | bytes 3000000 | tf_op jit(solution)/shard_map/merge/pallas_call | solution.py:267
  (52 shorter events, 18.1 us)
Async XLA Ops:
  6.5 118.5 %all-gather.2.cloned.1.call-start = ((), (), s32[]{:S(2)}) async-start(), calls=%async_computation | async-start | bytes 13312000 | tf_op jit(solution)/shard_map/all_gather | solution.py:298
  8.4 6.4 %collective-permute-start.3 = (bf16[224,256]{1,0:T(8,128)(2,1)S(1)}, bf16[224,256]{1,0:T(8,128)(2,1)S(1)}, u32[]{:S(2)}, u32[]{:S(2)}) collective-permute-start(bf16[224,256]{1,0:T(8,128)(2,1)S(1)} %pad_maximum_fusion.2), channel_id=1, source_target_pairs={{0,1},{1,2},{2,3},{3,0},{4,5},{5,6},{6,7},{7,4},{8,9},{9,10},{10,1... | collective-permute-start | bytes 344072 | tf_op jit(solution)/shard_map/ppermute | solution.py:20
  10.6 4.1 %collective-permute-start.4 = (bf16[224,256]{1,0:T(8,128)(2,1)S(1)}, bf16[224,256]{1,0:T(8,128)(2,1)S(1)}, u32[]{:S(2)}, u32[]{:S(2)}) collective-permute-start(bf16[224,256]{1,0:T(8,128)(2,1)S(1)} %pad_maximum_fusion.3), channel_id=1, source_target_pairs={{0,3},{1,0},{2,1},{3,2},{4,7},{5,4},{6,5},{7,6},{8,11},{9,8},{10,9... | collective-permute-start | bytes 344072 | tf_op jit(solution)/shard_map/ppermute | solution.py:20
  12.1 6.1 %collective-permute-start.5 = (bf16[224,256]{1,0:T(8,128)(2,1)S(1)}, bf16[224,256]{1,0:T(8,128)(2,1)S(1)}, u32[]{:S(2)}, u32[]{:S(2)}) collective-permute-start(bf16[224,256]{1,0:T(8,128)(2,1)S(1)} %pad_maximum_fusion.4), channel_id=1, source_target_pairs={{0,2},{1,3},{2,0},{3,1},{4,6},{5,7},{6,4},{7,5},{8,10},{9,11},{10,... | collective-permute-start | bytes 344072 | tf_op jit(solution)/shard_map/ppermute | solution.py:20
  18.3 12.5 %collective-permute-start.6 = (bf16[4,224,256]{2,1,0:T(8,128)(2,1)S(1)}, bf16[4,224,256]{2,1,0:T(8,128)(2,1)S(1)}, u32[]{:S(2)}, u32[]{:S(2)}) collective-permute-start(bf16[4,224,256]{2,1,0:T(8,128)(2,1)S(1)} %pad_maximum_fusion.refs_4_), channel_id=1, source_target_pairs={{0,4},{4,8},{8,12},{12,0},{1,5},{5,9},{9,13},{13,1},{2,6},{6,10},{... | collective-permute-start | bytes 1376264 | tf_op jit(solution)/shard_map/ppermute | solution.py:20
  19.5 12.0 %collective-permute-start.7 = (bf16[4,224,256]{2,1,0:T(8,128)(2,1)S(1)}, bf16[4,224,256]{2,1,0:T(8,128)(2,1)S(1)}, u32[]{:S(2)}, u32[]{:S(2)}) collective-permute-start(bf16[4,224,256]{2,1,0:T(8,128)(2,1)S(1)} %pad_maximum_fusion.refs_4_), channel_id=1, source_target_pairs={{0,12},{4,0},{8,4},{12,8},{1,13},{5,1},{9,5},{13,9},{2,14},{6,2},{... | collective-permute-start | bytes 1376264 | tf_op jit(solution)/shard_map/ppermute | solution.py:20
  21.0 16.0 %collective-permute-start.10 = (bf16[4,224,256]{2,1,0:T(8,128)(2,1)S(1)}, bf16[4,224,256]{2,1,0:T(8,128)(2,1)S(1)}, u32[]{:S(2)}, u32[]{:S(2)}) collective-permute-start(bf16[4,224,256]{2,1,0:T(8,128)(2,1)S(1)} %pad_maximum_fusion.refs_4_), channel_id=1, source_target_pairs={{0,16},{16,0},{1,17},{17,1},{2,18},{18,2},{3,19},{19,3},{4,20},{20... | collective-permute-start | bytes 1376264 | tf_op jit(solution)/shard_map/ppermute | solution.py:20
  31.5 8.3 %collective-permute-start.8 = (bf16[2,224,256]{2,1,0:T(8,128)(2,1)}, bf16[2,224,256]{2,1,0:T(8,128)(2,1)S(1)}, u32[]{:S(2)}, u32[]{:S(2)}) collective-permute-start(bf16[2,224,256]{2,1,0:T(8,128)(2,1)} %slice.8), channel_id=1, source_target_pairs={{0,4},{4,8},{8,12},{12,0},{1,5},{5,9},{9,13},{13,1},{2,6},{6,10},{... | collective-permute-start | bytes 688136 | tf_op jit(solution)/shard_map/ppermute | solution.py:20
  32.2 7.6 %collective-permute-start.9 = (bf16[2,224,256]{2,1,0:T(8,128)(2,1)}, bf16[2,224,256]{2,1,0:T(8,128)(2,1)S(1)}, u32[]{:S(2)}, u32[]{:S(2)}) collective-permute-start(bf16[2,224,256]{2,1,0:T(8,128)(2,1)} %slice.9), channel_id=1, source_target_pairs={{0,12},{4,0},{8,4},{12,8},{1,13},{5,1},{9,5},{13,9},{2,14},{6,2},{... | collective-permute-start | bytes 688136 | tf_op jit(solution)/shard_map/ppermute | solution.py:20
  34.9 11.3 %copy-start.6 = (s32[1,64]{1,0:T(1,128)S(1)}, s32[1,64]{1,0:T(1,128)}, u32[]{:S(2)}) copy-start(s32[1,64]{1,0:T(1,128)} %param.11) | copy-start | bytes 772
  37.1 7.7 %collective-permute-start = (bf16[224,640]{1,0:T(8,128)(2,1)S(1)}, bf16[224,640]{1,0:T(8,128)(2,1)S(1)}, u32[]{:S(2)}, u32[]{:S(2)}) collective-permute-start(bf16[224,640]{1,0:T(8,128)(2,1)S(1)} %get-tuple-element.20), channel_id=1, source_target_pairs={{0,1},{1,2},{2,3},{3,0},{4,5},{5,6},{6,7},{7,4},{8,9},{9,10},{10,1... | collective-permute-start | bytes 860168 | tf_op jit(solution)/shard_map/ppermute | solution.py:20
  37.1 22.3 %collective-permute-start.11 = (bf16[4,224,256]{2,1,0:T(8,128)(2,1)S(1)}, bf16[4,224,256]{2,1,0:T(8,128)(2,1)S(1)}, u32[]{:S(2)}, u32[]{:S(2)}) collective-permute-start(bf16[4,224,256]{2,1,0:T(8,128)(2,1)S(1)} %collective-permute-done.10.refs_9_), channel_id=1, source_target_pairs={{0,4},{4,8},{8,12},{12,0},{1,5},{5,9},{9,13},{13,1},{2,6},{6,10},{... | collective-permute-start | bytes 1376264 | tf_op jit(solution)/shard_map/ppermute | solution.py:20
  37.2 22.2 %collective-permute-start.12 = (bf16[4,224,256]{2,1,0:T(8,128)(2,1)S(1)}, bf16[4,224,256]{2,1,0:T(8,128)(2,1)S(1)}, u32[]{:S(2)}, u32[]{:S(2)}) collective-permute-start(bf16[4,224,256]{2,1,0:T(8,128)(2,1)S(1)} %collective-permute-done.10.refs_9_), channel_id=1, source_target_pairs={{0,12},{4,0},{8,4},{12,8},{1,13},{5,1},{9,5},{13,9},{2,14},{6,2},{... | collective-permute-start | bytes 1376264 | tf_op jit(solution)/shard_map/ppermute | solution.py:20
  40.7 18.7 %collective-permute-start.13 = (bf16[4,224,256]{2,1,0:T(8,128)(2,1)}, bf16[4,224,256]{2,1,0:T(8,128)(2,1)}, u32[]{:S(2)}, u32[]{:S(2)}) collective-permute-start(bf16[4,224,256]{2,1,0:T(8,128)(2,1)} %pad_maximum_fusion.1), channel_id=1, source_target_pairs={{0,16},{16,0},{1,17},{17,1},{2,18},{18,2},{3,19},{19,3},{4,20},{20... | collective-permute-start | bytes 1376264 | tf_op jit(solution)/shard_map/ppermute | solution.py:20
  42.2 13.2 %collective-permute-start.1 = (bf16[224,640]{1,0:T(8,128)(2,1)}, bf16[224,640]{1,0:T(8,128)(2,1)}, u32[]{:S(2)}, u32[]{:S(2)}) collective-permute-start(bf16[224,640]{1,0:T(8,128)(2,1)} %get-tuple-element.22), channel_id=1, source_target_pairs={{0,3},{1,0},{2,1},{3,2},{4,7},{5,4},{6,5},{7,6},{8,11},{9,8},{10,9... | collective-permute-start | bytes 860168 | tf_op jit(solution)/shard_map/ppermute | solution.py:20
  45.5 13.9 %collective-permute-start.2 = (bf16[224,640]{1,0:T(8,128)(2,1)}, bf16[224,640]{1,0:T(8,128)(2,1)}, u32[]{:S(2)}, u32[]{:S(2)}) collective-permute-start(bf16[224,640]{1,0:T(8,128)(2,1)} %get-tuple-element.19), channel_id=1, source_target_pairs={{0,2},{1,3},{2,0},{3,1},{4,6},{5,7},{6,4},{7,5},{8,10},{9,11},{10,... | collective-permute-start | bytes 860168 | tf_op jit(solution)/shard_map/ppermute | solution.py:20
  76.6 17.9 %collective-permute-start.14 = (bf16[224,640]{1,0:T(8,128)(2,1)S(1)}, bf16[224,640]{1,0:T(8,128)(2,1)S(1)}, u32[]{:S(2)}, u32[]{:S(2)}) collective-permute-start(bf16[224,640]{1,0:T(8,128)(2,1)S(1)} %get-tuple-element.12), channel_id=1, source_target_pairs={{0,1},{1,2},{2,3},{3,0},{4,5},{5,6},{6,7},{7,4},{8,9},{9,10},{10,1... | collective-permute-start | bytes 860168 | tf_op jit(solution)/shard_map/ppermute | solution.py:20
  81.2 17.7 %collective-permute-start.15 = (bf16[224,640]{1,0:T(8,128)(2,1)S(1)}, bf16[224,640]{1,0:T(8,128)(2,1)S(1)}, u32[]{:S(2)}, u32[]{:S(2)}) collective-permute-start(bf16[224,640]{1,0:T(8,128)(2,1)S(1)} %get-tuple-element.13), channel_id=1, source_target_pairs={{0,3},{1,0},{2,1},{3,2},{4,7},{5,4},{6,5},{7,6},{8,11},{9,8},{10,9... | collective-permute-start | bytes 860168 | tf_op jit(solution)/shard_map/ppermute | solution.py:20
  82.1 25.7 %collective-permute-start.16 = (bf16[224,640]{1,0:T(8,128)(2,1)S(1)}, bf16[224,640]{1,0:T(8,128)(2,1)S(1)}, u32[]{:S(2)}, u32[]{:S(2)}) collective-permute-start(bf16[224,640]{1,0:T(8,128)(2,1)S(1)} %get-tuple-element.14), channel_id=1, source_target_pairs={{0,2},{1,3},{2,0},{3,1},{4,6},{5,7},{6,4},{7,5},{8,10},{9,11},{10,... | collective-permute-start | bytes 860168 | tf_op jit(solution)/shard_map/ppermute | solution.py:20
  83.2 28.6 %collective-permute-start.17 = (bf16[224,640]{1,0:T(8,128)(2,1)S(1)}, bf16[224,640]{1,0:T(8,128)(2,1)S(1)}, u32[]{:S(2)}, u32[]{:S(2)}) collective-permute-start(bf16[224,640]{1,0:T(8,128)(2,1)S(1)} %get-tuple-element.11.refs_0_), channel_id=1, source_target_pairs={{0,32},{32,0},{1,33},{33,1},{2,34},{34,2},{3,35},{35,3},{4,36},{36... | collective-permute-start | bytes 860168 | tf_op jit(solution)/shard_map/ppermute | solution.py:20
  94.5 17.3 %collective-permute-start.18 = (bf16[224,640]{1,0:T(8,128)(2,1)S(1)}, bf16[224,640]{1,0:T(8,128)(2,1)S(1)}, u32[]{:S(2)}, u32[]{:S(2)}) collective-permute-start(bf16[224,640]{1,0:T(8,128)(2,1)S(1)} %collective-permute-done.14.refs_1_), channel_id=1, source_target_pairs={{0,32},{32,0},{1,33},{33,1},{2,34},{34,2},{3,35},{35,3},{4,36},{36... | collective-permute-start | bytes 860168 | tf_op jit(solution)/shard_map/ppermute | solution.py:20
  98.9 12.9 %collective-permute-start.19 = (bf16[224,640]{1,0:T(8,128)(2,1)S(1)}, bf16[224,640]{1,0:T(8,128)(2,1)S(1)}, u32[]{:S(2)}, u32[]{:S(2)}) collective-permute-start(bf16[224,640]{1,0:T(8,128)(2,1)S(1)} %collective-permute-done.15.refs_2_), channel_id=1, source_target_pairs={{0,32},{32,0},{1,33},{33,1},{2,34},{34,2},{3,35},{35,3},{4,36},{36... | collective-permute-start | bytes 860168 | tf_op jit(solution)/shard_map/ppermute | solution.py:20
  107.8 5.3 %collective-permute-start.20 = (bf16[224,640]{1,0:T(8,128)(2,1)S(1)}, bf16[224,640]{1,0:T(8,128)(2,1)S(1)}, u32[]{:S(2)}, u32[]{:S(2)}) collective-permute-start(bf16[224,640]{1,0:T(8,128)(2,1)S(1)} %collective-permute-done.16.refs_3_), channel_id=1, source_target_pairs={{0,32},{32,0},{1,33},{33,1},{2,34},{34,2},{3,35},{35,3},{4,36},{36... | collective-permute-start | bytes 860168 | tf_op jit(solution)/shard_map/ppermute | solution.py:20
  136.7 3.1 %collective-permute-start.21 = (bf16[2,224,1280]{2,1,0:T(8,128)(2,1)S(1)}, bf16[2,224,1280]{2,1,0:T(8,128)(2,1)S(1)}, u32[]{:S(2)}, u32[]{:S(2)}) collective-permute-start(bf16[2,224,1280]{2,1,0:T(8,128)(2,1)S(1)} %get-tuple-element.15), channel_id=1, source_target_pairs={{0,32},{32,0},{1,33},{33,1},{2,34},{34,2},{3,35},{35,3},{4,36},{36... | collective-permute-start | bytes 3440648 | tf_op jit(solution)/shard_map/ppermute | solution.py:20
  (6 other events, 25.3 us)
Sparse Core Ops, SparseCore 0:
  10.2 114.7 all-gather.1

commit v4 on v3

--- a/solution.py
+++ b/solution.py
@@ -203,16 +203,18 @@
 
 def project_kernel(base, table, *refs):
     att_refs, weights = refs[:8], refs[8]
-    own_out, other_out, att = refs[9:]
+    own_out, other_out, att, sem = refs[9:]
     tok, wide = att_refs[0].shape
 
     @pl.when(pl.program_id(0) == 0)
     def _():
-        for who in range(2):
-            for j in range(4):
-                head = wrap(table[base + 4] + SHIFTS[j])
-                at = pl.multiple_of(head * wide, HD)
-                att[pl.ds(who * tok, tok), pl.ds(at, wide)] = att_refs[4 * who + j][...]
+        here = pl.multiple_of(table[base + 4] * wide, HD)
+        own = pltpu.make_async_copy(att_refs[0], att.at[pl.ds(0, tok), pl.ds(here, wide)], sem)
+        own.start()
+        for i in range(1, 8):
+            at = pl.multiple_of(wrap(table[base + 4] + SHIFTS[i % 4]) * wide, HD)
+            att[pl.ds(i // 4 * tok, tok), pl.ds(at, wide)] = att_refs[i][...]
+        own.wait()
 
     got = jnp.dot(att[...], weights[...], preferred_element_type=jnp.float32)
     got = got.astype(own_out.dtype)
@@ -233,12 +235,17 @@
         grid_spec=pltpu.PrefetchScalarGridSpec(
             num_scalar_prefetch=1,
             grid=(2,),
-            in_specs=[piece] * 8 + [pl.BlockSpec((rows, cols), lambda i, *_: (i, 0))],
+            in_specs=[pl.BlockSpec(memory_space=pl.ANY)]
+            + [piece] * 7
+            + [pl.BlockSpec((rows, cols), lambda i, *_: (i, 0))],
             out_specs=[
                 pl.BlockSpec((tok, cols), lambda i, table: (0, i * 2 + table[base + 6])),
                 pl.BlockSpec((1, tok, cols), lambda i, *_: (i, 0, 0)),
             ],
-            scratch_shapes=[pltpu.VMEM((2 * tok, rows), jnp.bfloat16)],
+            scratch_shapes=[
+                pltpu.VMEM((2 * tok, rows), jnp.bfloat16),
+                pltpu.SemaphoreType.DMA,
+            ],
         ),
         compiler_params=pltpu.CompilerParams(vmem_limit_bytes=48 * 2**20),
         cost_estimate=pl.CostEstimate(

time: 149 us -> 149 us (level)
  waiting for transfers between devices: 55.4 us -> 68.6 us
  starting transfers between devices: 39.9 us -> 26.8 us
    ppermute x22, starting transfers between devices: 39.9 us -> 26.8 us  [shifted(): lax.ppermute(array, axis, [(i, (i + step) % size) for i in range(size)])]
    ppermute x22, waiting for transfers between devices: 42.7 us -> 51.9 us  [shifted(): lax.ppermute(array, axis, [(i, (i + step) % size) for i in range(size)])]
    all_gather x1, waiting for transfers between devices: 12 us -> 16 us  [per_device(): lax.all_gather(out_weight, ('zh', 'zl', 'x', 'y'), axis=0, tiled=True)]
  transfers between devices with their start and end apart: 23 -> 23, of which waited for: 10 -> 11; matrix products, arithmetic and copies ran while one was open for 5% -> 5% of each run, Pallas kernels for 11% -> 11%
where the time goes in v4:
time: 149 us; the launch traced here: 148 us
  waiting for transfers between devices  68.6 us (46%)
  Pallas kernels  28.4 us (19%)
  starting transfers between devices  26.8 us (18%)
  between operations  13.5 us (9%)
  local copies, waits for them, and re-layouts  9.33 us (6%)
  other arithmetic  1.65 us (1%)
    ppermute x22, waiting for transfers between devices, shifted(): lax.ppermute(array, axis, [(i, (i + step) % size) for i in range(size)])  51.9 us
    ppermute x22, starting transfers between devices, shifted(): lax.ppermute(array, axis, [(i, (i + step) % size) for i in range(size)])  26.8 us
    pallas_call x1, Pallas kernels, attention(): pl.pallas_call(functools.partial(attention_kernel, groups, sec, nsec, shi...  16.2 us
    all_gather x1, waiting for transfers between devices, per_device(): lax.all_gather(out_weight, ('zh', 'zl', 'x', 'y'), axis=0, tiled=True)  16 us
    pallas_call x1, Pallas kernels, project(): pl.pallas_call(functools.partial(project_kernel, base), out_shape=[jax.Sh...  10.7 us
    unnamed x14, local copies, waits for them, and re-layouts  3.36 us
    dynamic_slice x2, local copies, waits for them, and re-layouts, head_slice(): return lax.dynamic_slice_in_dim(array[0], wrap(y + shift) * wide, wide, 1)  3.24 us
  transfers between devices with their start and end apart: 23, of which 11 were waited for; matrix products, arithmetic and copies ran while one was open for 5% of the time, Pallas kernels for 11%

profile of v4, /device:TPU:1, one launch (start us, length us, event | category | flops | bytes accessed | tf_op | source)
XLA Modules:
  0.0 148.3 jit_solution(11854223843128189757)
XLA Ops:
  8.4 2.2 %collective-permute-start.3 = (bf16[224,256]{1,0:T(8,128)(2,1)S(1)}, bf16[224,256]{1,0:T(8,128)(2,1)S(1)}, u32[]{:S(2)}, u32[]{:S(2)}) collective-permute-start(bf16[224,256]{1,0:T(8,128)(2,1)S(1)} %pad_maximum_fusion.2), channel_id=1, source_target_pairs={{0,1},{1,2},{2,3},{3,0},{4,5},{5,6},{6,7},{7,4},{8,9},{9,10},{10,1... | collective-permute-start | bytes 344072 | tf_op jit(solution)/shard_map/ppermute | solution.py:20
  10.6 1.5 %collective-permute-start.4 = (bf16[224,256]{1,0:T(8,128)(2,1)S(1)}, bf16[224,256]{1,0:T(8,128)(2,1)S(1)}, u32[]{:S(2)}, u32[]{:S(2)}) collective-permute-start(bf16[224,256]{1,0:T(8,128)(2,1)S(1)} %pad_maximum_fusion.3), channel_id=1, source_target_pairs={{0,3},{1,0},{2,1},{3,2},{4,7},{5,4},{6,5},{7,6},{8,11},{9,8},{10,9... | collective-permute-start | bytes 344072 | tf_op jit(solution)/shard_map/ppermute | solution.py:20
  12.1 1.7 %collective-permute-start.5 = (bf16[224,256]{1,0:T(8,128)(2,1)S(1)}, bf16[224,256]{1,0:T(8,128)(2,1)S(1)}, u32[]{:S(2)}, u32[]{:S(2)}) collective-permute-start(bf16[224,256]{1,0:T(8,128)(2,1)S(1)} %pad_maximum_fusion.4), channel_id=1, source_target_pairs={{0,2},{1,3},{2,0},{3,1},{4,6},{5,7},{6,4},{7,5},{8,10},{9,11},{10,... | collective-permute-start | bytes 344072 | tf_op jit(solution)/shard_map/ppermute | solution.py:20
  14.7 3.5 %collective-permute-done.5 = bf16[224,256]{1,0:T(8,128)(2,1)S(1)} collective-permute-done((bf16[224,256]{1,0:T(8,128)(2,1)S(1)}, bf16[224,256]{1,0:T(8,128)(2,1)S(1)}, u32[]{:S(2)}, u32[]{:S(2)}) %collective-permute-start.5) | collective-permute-done | bytes 114720 | tf_op jit(solution)/shard_map/ppermute | solution.py:20
  19.5 1.5 %collective-permute-start.7 = (bf16[4,224,256]{2,1,0:T(8,128)(2,1)S(1)}, bf16[4,224,256]{2,1,0:T(8,128)(2,1)S(1)}, u32[]{:S(2)}, u32[]{:S(2)}) collective-permute-start(bf16[4,224,256]{2,1,0:T(8,128)(2,1)S(1)} %pad_maximum_fusion.refs_4_), channel_id=1, source_target_pairs={{0,12},{4,0},{8,4},{12,8},{1,13},{5,1},{9,5},{13,9},{2,14},{6,2},{... | collective-permute-start | bytes 1376264 | tf_op jit(solution)/shard_map/ppermute | solution.py:20
  21.0 1.6 %collective-permute-start.10 = (bf16[4,224,256]{2,1,0:T(8,128)(2,1)S(1)}, bf16[4,224,256]{2,1,0:T(8,128)(2,1)S(1)}, u32[]{:S(2)}, u32[]{:S(2)}) collective-permute-start(bf16[4,224,256]{2,1,0:T(8,128)(2,1)S(1)} %pad_maximum_fusion.refs_4_), channel_id=1, source_target_pairs={{0,16},{16,0},{1,17},{17,1},{2,18},{18,2},{3,19},{19,3},{4,20},{20... | collective-permute-start | bytes 1376264 | tf_op jit(solution)/shard_map/ppermute | solution.py:20
  22.6 8.2 %collective-permute-done.6.refs_5_ = bf16[4,224,256]{2,1,0:T(8,128)(2,1)S(1)} collective-permute-done((bf16[4,224,256]{2,1,0:T(8,128)(2,1)S(1)}, bf16[4,224,256]{2,1,0:T(8,128)(2,1)S(1)}, u32[]{:S(2)}, u32[]{:S(2)}) %collective-permute-start.6) | collective-permute-done | bytes 458784 | tf_op jit(solution)/shard_map/ppermute | solution.py:20
  32.2 2.7 %collective-permute-start.9 = (bf16[2,224,256]{2,1,0:T(8,128)(2,1)}, bf16[2,224,256]{2,1,0:T(8,128)(2,1)S(1)}, u32[]{:S(2)}, u32[]{:S(2)}) collective-permute-start(bf16[2,224,256]{2,1,0:T(8,128)(2,1)} %slice.9), channel_id=1, source_target_pairs={{0,12},{4,0},{8,4},{12,8},{1,13},{5,1},{9,5},{13,9},{2,14},{6,2},{... | collective-permute-start | bytes 688136 | tf_op jit(solution)/shard_map/ppermute | solution.py:20
  34.9 2.2 %dynamic-slice_bitcast_fusion = (bf16[224,640]{1,0:T(8,128)(2,1)}, bf16[224,640]{1,0:T(8,128)(2,1)S(1)}, bf16[224,640]{1,0:T(8,128)(2,1)S(1)}, bf16[224,640]{1,0:T(8,128)(2,1)}) fusion(bf16[1,224,2560]{2,1,0:T(8,128)(2,1)} %param.7, s32[]{:T(128)S(6)} %select_n.31, s32[]{:T(128)S(6)} %select_n.29, s32[]{:T(128)S(6)} %select_n.28, s32[]{:T(128)S(6)} %select_n.30), kind=kLoop, calls=%fused_computation.2 | loop fusion | bytes 2293776 | tf_op jit(solution)/shard_map/dynamic_slice | solution.py:303
  37.2 2.7 %collective-permute-start.12 = (bf16[4,224,256]{2,1,0:T(8,128)(2,1)S(1)}, bf16[4,224,256]{2,1,0:T(8,128)(2,1)S(1)}, u32[]{:S(2)}, u32[]{:S(2)}) collective-permute-start(bf16[4,224,256]{2,1,0:T(8,128)(2,1)S(1)} %collective-permute-done.10.refs_9_), channel_id=1, source_target_pairs={{0,12},{4,0},{8,4},{12,8},{1,13},{5,1},{9,5},{13,9},{2,14},{6,2},{... | collective-permute-start | bytes 1376264 | tf_op jit(solution)/shard_map/ppermute | solution.py:20
  40.7 1.5 %collective-permute-start.13 = (bf16[4,224,256]{2,1,0:T(8,128)(2,1)}, bf16[4,224,256]{2,1,0:T(8,128)(2,1)}, u32[]{:S(2)}, u32[]{:S(2)}) collective-permute-start(bf16[4,224,256]{2,1,0:T(8,128)(2,1)} %pad_maximum_fusion.1), channel_id=1, source_target_pairs={{0,16},{16,0},{1,17},{17,1},{2,18},{18,2},{3,19},{19,3},{4,20},{20... | collective-permute-start | bytes 1376264 | tf_op jit(solution)/shard_map/ppermute | solution.py:20
  42.2 2.6 %collective-permute-start.1 = (bf16[224,640]{1,0:T(8,128)(2,1)}, bf16[224,640]{1,0:T(8,128)(2,1)}, u32[]{:S(2)}, u32[]{:S(2)}) collective-permute-start(bf16[224,640]{1,0:T(8,128)(2,1)} %get-tuple-element.22), channel_id=1, source_target_pairs={{0,3},{1,0},{2,1},{3,2},{4,7},{5,4},{6,5},{7,6},{8,11},{9,8},{10,9... | collective-permute-start | bytes 860168 | tf_op jit(solution)/shard_map/ppermute | solution.py:20
  46.3 1.3 concatenate.18.table
  47.6 7.8 %collective-permute-done.1.refs_2_ = bf16[224,640]{1,0:T(8,128)(2,1)} collective-permute-done((bf16[224,640]{1,0:T(8,128)(2,1)}, bf16[224,640]{1,0:T(8,128)(2,1)}, u32[]{:S(2)}, u32[]{:S(2)}) %collective-permute-start.1) | collective-permute-done | bytes 286752 | tf_op jit(solution)/shard_map/ppermute | solution.py:20
  55.3 4.0 %collective-permute-done.2.refs_3_ = bf16[224,640]{1,0:T(8,128)(2,1)} collective-permute-done((bf16[224,640]{1,0:T(8,128)(2,1)}, bf16[224,640]{1,0:T(8,128)(2,1)}, u32[]{:S(2)}, u32[]{:S(2)}) %collective-permute-start.2) | collective-permute-done | bytes 286752 | tf_op jit(solution)/shard_map/ppermute | solution.py:20
  60.3 16.2 %attend.1 = (bf16[224,640]{1,0:T(8,128)(2,1)S(1)}, bf16[224,640]{1,0:T(8,128)(2,1)S(1)}, bf16[224,640]{1,0:T(8,128)(2,1)S(1)}, bf16[224,640]{1,0:T(8,128)(2,1)S(1)}) custom-call(s32[135]{0:T(256)S(1)} %concatenate.18.table, bf16[224,640]{1,0:T(8,128)(2,1)S(1)} %get-tuple-element.21.refs_0_, bf16[224,640]{1,0:T(8,128)(2,1)S(1)} %copy-done.1, ...), custom_call_target="tpu_custom_call" | custom-call | flops 8000000000 | bytes 6000000 | tf_op jit(solution)/shard_map/attend/pallas_call | solution.py:181
  76.5 4.7 %collective-permute-start.14 = (bf16[224,640]{1,0:T(8,128)(2,1)S(1)}, bf16[224,640]{1,0:T(8,128)(2,1)S(1)}, u32[]{:S(2)}, u32[]{:S(2)}) collective-permute-start(bf16[224,640]{1,0:T(8,128)(2,1)S(1)} %get-tuple-element.12), channel_id=1, source_target_pairs={{0,1},{1,2},{2,3},{3,0},{4,5},{5,6},{6,7},{7,4},{8,9},{9,10},{10,1... | collective-permute-start | bytes 860168 | tf_op jit(solution)/shard_map/ppermute | solution.py:20
  83.9 11.1 %collective-permute-done.14.refs_1_ = bf16[224,640]{1,0:T(8,128)(2,1)S(1)} collective-permute-done((bf16[224,640]{1,0:T(8,128)(2,1)S(1)}, bf16[224,640]{1,0:T(8,128)(2,1)S(1)}, u32[]{:S(2)}, u32[]{:S(2)}) %collective-permute-start.14) | collective-permute-done | bytes 286752 | tf_op jit(solution)/shard_map/ppermute | solution.py:20
  96.3 11.2 %collective-permute-done.16.refs_3_ = bf16[224,640]{1,0:T(8,128)(2,1)S(1)} collective-permute-done((bf16[224,640]{1,0:T(8,128)(2,1)S(1)}, bf16[224,640]{1,0:T(8,128)(2,1)S(1)}, u32[]{:S(2)}, u32[]{:S(2)}) %collective-permute-start.16) | collective-permute-done | bytes 286752 | tf_op jit(solution)/shard_map/ppermute | solution.py:20
  107.5 1.5 %collective-permute-done.20.refs_7_ = bf16[224,640]{1,0:T(8,128)(2,1)S(1)} collective-permute-done((bf16[224,640]{1,0:T(8,128)(2,1)S(1)}, bf16[224,640]{1,0:T(8,128)(2,1)S(1)}, u32[]{:S(2)}, u32[]{:S(2)}) %collective-permute-start.20) | collective-permute-done | bytes 286752 | tf_op jit(solution)/shard_map/ppermute | solution.py:20
  109.0 16.0 %all-gather.2.cloned.1.call-done.refs_8_ = bf16[5120,1280]{1,0:T(8,128)(2,1)} async-done(((bf16[80,1280]{1,0:T(8,128)(2,1)}), bf16[5120,1280]{1,0:T(8,128)(2,1)}) %all-gather.2.cloned.1.call-update) | async-done | bytes 13107216 | tf_op jit(solution)/shard_map/all_gather | solution.py:305
  126.0 10.7 %project.1 = (bf16[224,5120]{1,0:T(8,128)(2,1)}, bf16[2,224,1280]{2,1,0:T(8,128)(2,1)S(1)}) custom-call(s32[135]{0:T(256)S(1)} %concatenate.18.table, bf16[224,640]{1,0:T(8,128)(2,1)S(1)} %copy-done.3, bf16[224,640]{1,0:T(8,128)(2,1)S(1)} %collective-permute-done.14.refs_1_, bf16[224,640]{1,0:T(8,128)(2,1)S(1)} %collective-permute-done.15.refs_2_, ...), custom_call_target="tpu_custom_call" | custom-call | flops 6000000000 | bytes 18000000 | tf_op jit(solution)/shard_map/project/pallas_call | solution.py:229
  137.5 2.4 %collective-permute-done.21.theirs = bf16[2,224,1280]{2,1,0:T(8,128)(2,1)S(1)} collective-permute-done((bf16[2,224,1280]{2,1,0:T(8,128)(2,1)S(1)}, bf16[2,224,1280]{2,1,0:T(8,128)(2,1)S(1)}, u32[]{:S(2)}, u32[]{:S(2)}) %collective-permute-start.21) | collective-permute-done | bytes 1146912 | tf_op jit(solution)/shard_map/ppermute | solution.py:20
  139.9 1.6 %merge.1 = bf16[224,5120]{1,0:T(8,128)(2,1)} custom-call(s32[135]{0:T(256)S(1)} %concatenate.18.table, bf16[2,224,1280]{2,1,0:T(8,128)(2,1)S(1)} %collective-permute-done.21.theirs, bf16[224,5120]{1,0:T(8,128)(2,1)} %get-tuple-element.16.whole), custom_call_target="tpu_custom_call", output_to_operand_aliasing={{}: (2, {})} | custom-call | bytes 3000000 | tf_op jit(solution)/shard_map/merge/pallas_call | solution.py:274
  (52 shorter events, 14.4 us)
Async XLA Ops:
  6.5 118.5 %all-gather.2.cloned.1.call-start = ((), (), s32[]{:S(2)}) async-start(), calls=%async_computation | async-start | bytes 13312000 | tf_op jit(solution)/shard_map/all_gather | solution.py:305
  8.4 6.4 %collective-permute-start.3 = (bf16[224,256]{1,0:T(8,128)(2,1)S(1)}, bf16[224,256]{1,0:T(8,128)(2,1)S(1)}, u32[]{:S(2)}, u32[]{:S(2)}) collective-permute-start(bf16[224,256]{1,0:T(8,128)(2,1)S(1)} %pad_maximum_fusion.2), channel_id=1, source_target_pairs={{0,1},{1,2},{2,3},{3,0},{4,5},{5,6},{6,7},{7,4},{8,9},{9,10},{10,1... | collective-permute-start | bytes 344072 | tf_op jit(solution)/shard_map/ppermute | solution.py:20
  10.6 4.1 %collective-permute-start.4 = (bf16[224,256]{1,0:T(8,128)(2,1)S(1)}, bf16[224,256]{1,0:T(8,128)(2,1)S(1)}, u32[]{:S(2)}, u32[]{:S(2)}) collective-permute-start(bf16[224,256]{1,0:T(8,128)(2,1)S(1)} %pad_maximum_fusion.3), channel_id=1, source_target_pairs={{0,3},{1,0},{2,1},{3,2},{4,7},{5,4},{6,5},{7,6},{8,11},{9,8},{10,9... | collective-permute-start | bytes 344072 | tf_op jit(solution)/shard_map/ppermute | solution.py:20
  12.1 6.1 %collective-permute-start.5 = (bf16[224,256]{1,0:T(8,128)(2,1)S(1)}, bf16[224,256]{1,0:T(8,128)(2,1)S(1)}, u32[]{:S(2)}, u32[]{:S(2)}) collective-permute-start(bf16[224,256]{1,0:T(8,128)(2,1)S(1)} %pad_maximum_fusion.4), channel_id=1, source_target_pairs={{0,2},{1,3},{2,0},{3,1},{4,6},{5,7},{6,4},{7,5},{8,10},{9,11},{10,... | collective-permute-start | bytes 344072 | tf_op jit(solution)/shard_map/ppermute | solution.py:20
  18.3 12.5 %collective-permute-start.6 = (bf16[4,224,256]{2,1,0:T(8,128)(2,1)S(1)}, bf16[4,224,256]{2,1,0:T(8,128)(2,1)S(1)}, u32[]{:S(2)}, u32[]{:S(2)}) collective-permute-start(bf16[4,224,256]{2,1,0:T(8,128)(2,1)S(1)} %pad_maximum_fusion.refs_4_), channel_id=1, source_target_pairs={{0,4},{4,8},{8,12},{12,0},{1,5},{5,9},{9,13},{13,1},{2,6},{6,10},{... | collective-permute-start | bytes 1376264 | tf_op jit(solution)/shard_map/ppermute | solution.py:20
  19.5 12.0 %collective-permute-start.7 = (bf16[4,224,256]{2,1,0:T(8,128)(2,1)S(1)}, bf16[4,224,256]{2,1,0:T(8,128)(2,1)S(1)}, u32[]{:S(2)}, u32[]{:S(2)}) collective-permute-start(bf16[4,224,256]{2,1,0:T(8,128)(2,1)S(1)} %pad_maximum_fusion.refs_4_), channel_id=1, source_target_pairs={{0,12},{4,0},{8,4},{12,8},{1,13},{5,1},{9,5},{13,9},{2,14},{6,2},{... | collective-permute-start | bytes 1376264 | tf_op jit(solution)/shard_map/ppermute | solution.py:20
  21.0 16.0 %collective-permute-start.10 = (bf16[4,224,256]{2,1,0:T(8,128)(2,1)S(1)}, bf16[4,224,256]{2,1,0:T(8,128)(2,1)S(1)}, u32[]{:S(2)}, u32[]{:S(2)}) collective-permute-start(bf16[4,224,256]{2,1,0:T(8,128)(2,1)S(1)} %pad_maximum_fusion.refs_4_), channel_id=1, source_target_pairs={{0,16},{16,0},{1,17},{17,1},{2,18},{18,2},{3,19},{19,3},{4,20},{20... | collective-permute-start | bytes 1376264 | tf_op jit(solution)/shard_map/ppermute | solution.py:20
  31.5 8.3 %collective-permute-start.8 = (bf16[2,224,256]{2,1,0:T(8,128)(2,1)}, bf16[2,224,256]{2,1,0:T(8,128)(2,1)S(1)}, u32[]{:S(2)}, u32[]{:S(2)}) collective-permute-start(bf16[2,224,256]{2,1,0:T(8,128)(2,1)} %slice.8), channel_id=1, source_target_pairs={{0,4},{4,8},{8,12},{12,0},{1,5},{5,9},{9,13},{13,1},{2,6},{6,10},{... | collective-permute-start | bytes 688136 | tf_op jit(solution)/shard_map/ppermute | solution.py:20
  32.2 7.6 %collective-permute-start.9 = (bf16[2,224,256]{2,1,0:T(8,128)(2,1)}, bf16[2,224,256]{2,1,0:T(8,128)(2,1)S(1)}, u32[]{:S(2)}, u32[]{:S(2)}) collective-permute-start(bf16[2,224,256]{2,1,0:T(8,128)(2,1)} %slice.9), channel_id=1, source_target_pairs={{0,12},{4,0},{8,4},{12,8},{1,13},{5,1},{9,5},{13,9},{2,14},{6,2},{... | collective-permute-start | bytes 688136 | tf_op jit(solution)/shard_map/ppermute | solution.py:20
  34.9 11.3 %copy-start.6 = (s32[1,64]{1,0:T(1,128)S(1)}, s32[1,64]{1,0:T(1,128)}, u32[]{:S(2)}) copy-start(s32[1,64]{1,0:T(1,128)} %param.11) | copy-start | bytes 772
  37.1 7.7 %collective-permute-start = (bf16[224,640]{1,0:T(8,128)(2,1)S(1)}, bf16[224,640]{1,0:T(8,128)(2,1)S(1)}, u32[]{:S(2)}, u32[]{:S(2)}) collective-permute-start(bf16[224,640]{1,0:T(8,128)(2,1)S(1)} %get-tuple-element.20), channel_id=1, source_target_pairs={{0,1},{1,2},{2,3},{3,0},{4,5},{5,6},{6,7},{7,4},{8,9},{9,10},{10,1... | collective-permute-start | bytes 860168 | tf_op jit(solution)/shard_map/ppermute | solution.py:20
  37.1 22.3 %collective-permute-start.11 = (bf16[4,224,256]{2,1,0:T(8,128)(2,1)S(1)}, bf16[4,224,256]{2,1,0:T(8,128)(2,1)S(1)}, u32[]{:S(2)}, u32[]{:S(2)}) collective-permute-start(bf16[4,224,256]{2,1,0:T(8,128)(2,1)S(1)} %collective-permute-done.10.refs_9_), channel_id=1, source_target_pairs={{0,4},{4,8},{8,12},{12,0},{1,5},{5,9},{9,13},{13,1},{2,6},{6,10},{... | collective-permute-start | bytes 1376264 | tf_op jit(solution)/shard_map/ppermute | solution.py:20
  37.2 22.2 %collective-permute-start.12 = (bf16[4,224,256]{2,1,0:T(8,128)(2,1)S(1)}, bf16[4,224,256]{2,1,0:T(8,128)(2,1)S(1)}, u32[]{:S(2)}, u32[]{:S(2)}) collective-permute-start(bf16[4,224,256]{2,1,0:T(8,128)(2,1)S(1)} %collective-permute-done.10.refs_9_), channel_id=1, source_target_pairs={{0,12},{4,0},{8,4},{12,8},{1,13},{5,1},{9,5},{13,9},{2,14},{6,2},{... | collective-permute-start | bytes 1376264 | tf_op jit(solution)/shard_map/ppermute | solution.py:20
  40.7 18.7 %collective-permute-start.13 = (bf16[4,224,256]{2,1,0:T(8,128)(2,1)}, bf16[4,224,256]{2,1,0:T(8,128)(2,1)}, u32[]{:S(2)}, u32[]{:S(2)}) collective-permute-start(bf16[4,224,256]{2,1,0:T(8,128)(2,1)} %pad_maximum_fusion.1), channel_id=1, source_target_pairs={{0,16},{16,0},{1,17},{17,1},{2,18},{18,2},{3,19},{19,3},{4,20},{20... | collective-permute-start | bytes 1376264 | tf_op jit(solution)/shard_map/ppermute | solution.py:20
  42.2 13.2 %collective-permute-start.1 = (bf16[224,640]{1,0:T(8,128)(2,1)}, bf16[224,640]{1,0:T(8,128)(2,1)}, u32[]{:S(2)}, u32[]{:S(2)}) collective-permute-start(bf16[224,640]{1,0:T(8,128)(2,1)} %get-tuple-element.22), channel_id=1, source_target_pairs={{0,3},{1,0},{2,1},{3,2},{4,7},{5,4},{6,5},{7,6},{8,11},{9,8},{10,9... | collective-permute-start | bytes 860168 | tf_op jit(solution)/shard_map/ppermute | solution.py:20
  45.5 13.9 %collective-permute-start.2 = (bf16[224,640]{1,0:T(8,128)(2,1)}, bf16[224,640]{1,0:T(8,128)(2,1)}, u32[]{:S(2)}, u32[]{:S(2)}) collective-permute-start(bf16[224,640]{1,0:T(8,128)(2,1)} %get-tuple-element.19), channel_id=1, source_target_pairs={{0,2},{1,3},{2,0},{3,1},{4,6},{5,7},{6,4},{7,5},{8,10},{9,11},{10,... | collective-permute-start | bytes 860168 | tf_op jit(solution)/shard_map/ppermute | solution.py:20
  76.5 18.5 %collective-permute-start.14 = (bf16[224,640]{1,0:T(8,128)(2,1)S(1)}, bf16[224,640]{1,0:T(8,128)(2,1)S(1)}, u32[]{:S(2)}, u32[]{:S(2)}) collective-permute-start(bf16[224,640]{1,0:T(8,128)(2,1)S(1)} %get-tuple-element.12), channel_id=1, source_target_pairs={{0,1},{1,2},{2,3},{3,0},{4,5},{5,6},{6,7},{7,4},{8,9},{9,10},{10,1... | collective-permute-start | bytes 860168 | tf_op jit(solution)/shard_map/ppermute | solution.py:20
  81.2 15.1 %collective-permute-start.15 = (bf16[224,640]{1,0:T(8,128)(2,1)S(1)}, bf16[224,640]{1,0:T(8,128)(2,1)S(1)}, u32[]{:S(2)}, u32[]{:S(2)}) collective-permute-start(bf16[224,640]{1,0:T(8,128)(2,1)S(1)} %get-tuple-element.13), channel_id=1, source_target_pairs={{0,3},{1,0},{2,1},{3,2},{4,7},{5,4},{6,5},{7,6},{8,11},{9,8},{10,9... | collective-permute-start | bytes 860168 | tf_op jit(solution)/shard_map/ppermute | solution.py:20
  82.1 25.4 %collective-permute-start.16 = (bf16[224,640]{1,0:T(8,128)(2,1)S(1)}, bf16[224,640]{1,0:T(8,128)(2,1)S(1)}, u32[]{:S(2)}, u32[]{:S(2)}) collective-permute-start(bf16[224,640]{1,0:T(8,128)(2,1)S(1)} %get-tuple-element.14), channel_id=1, source_target_pairs={{0,2},{1,3},{2,0},{3,1},{4,6},{5,7},{6,4},{7,5},{8,10},{9,11},{10,... | collective-permute-start | bytes 860168 | tf_op jit(solution)/shard_map/ppermute | solution.py:20
  83.2 24.3 %collective-permute-start.17 = (bf16[224,640]{1,0:T(8,128)(2,1)S(1)}, bf16[224,640]{1,0:T(8,128)(2,1)S(1)}, u32[]{:S(2)}, u32[]{:S(2)}) collective-permute-start(bf16[224,640]{1,0:T(8,128)(2,1)S(1)} %get-tuple-element.11.refs_0_), channel_id=1, source_target_pairs={{0,32},{32,0},{1,33},{33,1},{2,34},{34,2},{3,35},{35,3},{4,36},{36... | collective-permute-start | bytes 860168 | tf_op jit(solution)/shard_map/ppermute | solution.py:20
  95.0 12.4 %collective-permute-start.18 = (bf16[224,640]{1,0:T(8,128)(2,1)S(1)}, bf16[224,640]{1,0:T(8,128)(2,1)S(1)}, u32[]{:S(2)}, u32[]{:S(2)}) collective-permute-start(bf16[224,640]{1,0:T(8,128)(2,1)S(1)} %collective-permute-done.14.refs_1_), channel_id=1, source_target_pairs={{0,32},{32,0},{1,33},{33,1},{2,34},{34,2},{3,35},{35,3},{4,36},{36... | collective-permute-start | bytes 860168 | tf_op jit(solution)/shard_map/ppermute | solution.py:20
  96.3 11.2 %collective-permute-start.19 = (bf16[224,640]{1,0:T(8,128)(2,1)S(1)}, bf16[224,640]{1,0:T(8,128)(2,1)S(1)}, u32[]{:S(2)}, u32[]{:S(2)}) collective-permute-start(bf16[224,640]{1,0:T(8,128)(2,1)S(1)} %collective-permute-done.15.refs_2_), channel_id=1, source_target_pairs={{0,32},{32,0},{1,33},{33,1},{2,34},{34,2},{3,35},{35,3},{4,36},{36... | collective-permute-start | bytes 860168 | tf_op jit(solution)/shard_map/ppermute | solution.py:20
  107.5 1.6 %collective-permute-start.20 = (bf16[224,640]{1,0:T(8,128)(2,1)S(1)}, bf16[224,640]{1,0:T(8,128)(2,1)S(1)}, u32[]{:S(2)}, u32[]{:S(2)}) collective-permute-start(bf16[224,640]{1,0:T(8,128)(2,1)S(1)} %collective-permute-done.16.refs_3_), channel_id=1, source_target_pairs={{0,32},{32,0},{1,33},{33,1},{2,34},{34,2},{3,35},{35,3},{4,36},{36... | collective-permute-start | bytes 860168 | tf_op jit(solution)/shard_map/ppermute | solution.py:20
  136.7 3.2 %collective-permute-start.21 = (bf16[2,224,1280]{2,1,0:T(8,128)(2,1)S(1)}, bf16[2,224,1280]{2,1,0:T(8,128)(2,1)S(1)}, u32[]{:S(2)}, u32[]{:S(2)}) collective-permute-start(bf16[2,224,1280]{2,1,0:T(8,128)(2,1)S(1)} %get-tuple-element.15), channel_id=1, source_target_pairs={{0,32},{32,0},{1,33},{33,1},{2,34},{34,2},{3,35},{35,3},{4,36},{36... | collective-permute-start | bytes 3440648 | tf_op jit(solution)/shard_map/ppermute | solution.py:20
  (6 other events, 25.3 us)
Sparse Core Ops, SparseCore 0:
  10.2 114.7 all-gather.1
